TPU v7x, 256 devices: a whole 4x4x8 slice. The times are simulated.
256 devices in a mesh: tm: 32 (over z, x), chan: 8 (over y, core).
Axes of the slice: x: 4, y: 4, z: 8, core: 2. Of those that a mesh axis runs over, the one named last changes fastest.
Arguments:
- spectra: bfloat16 [16384, 8192], P('tm', 'chan'), may hold values from -6 to 6
- chan_weight: float32 [8192], P('chan'), may hold values from 0.25 to 4
- routes: int32 [1024, 1], P('tm'), may hold values from 0 to 31; in each aligned block of 32 rows (0 to 31, 32 to 63, ...) at most 2 rows name the same one
- offsets: int32 [16384], P('tm'), may hold values from 0 to 64
- kernel: bfloat16 [16], replicated, may hold values from 0.19921875 to 1
- gal_pix: int32 [256], replicated, may hold values from 0 to 2047
- gal_chan: int32 [256], replicated, may hold values from 64 to 8127, as said below
Outputs:
- sky_map: bfloat16 [2048, 8192], P('tm', 'chan')
- stacked: float32 [128], replicated
Inputs may be any that keep to these rules, and one draw needn't show every extreme that they name: `routes`: among the 32 blocks of one index of tm no tile is named more than 2 times; every tile is named by some block. `gal_chan`: channel of each galaxy's line centre.
All inputs are finite; a program needn't handle non-finite values.
Results may differ from a plain program's by a relative error of at most 0.012.
Values may be sent and summed in bfloat16 or wider, within the bound.
A program may use at most 64 MiB of HBM per device.

v0:
```python
import jax
import jax.numpy as jnp
import numpy as np
from jax import lax
from jax.experimental import pallas as pl
from jax.experimental.pallas import tpu as pltpu
from jax.sharding import PartitionSpec as P

KMODES = 8
MODES = 2 * KMODES
TP = 64
MARGIN = 8
SW = 64
TAPS = 16
NX = 4

highest = lax.Precision.HIGHEST
MESH = pl.DeviceIdType.MESH
f32 = jnp.float32
bf16 = jnp.bfloat16


def basis_table(total):
    orders = np.arange(1, KMODES + 1)[:, None]
    phase = (orders * np.arange(total)[None, :] % total) * (2 * np.pi / total)
    return np.concatenate([np.cos(phase), np.sin(phase)], axis=0).astype(np.float32)


def split3(value):
    high = value.astype(bf16)
    rest = value - high.astype(f32)
    mid = rest.astype(bf16)
    low = (rest - mid.astype(f32)).astype(bf16)
    return high, mid, low


def iota(shape, dim):
    return lax.broadcasted_iota(jnp.int32, shape, dim)


def make_kernel(tm_size, chan_size, rows, width, nblocks, ngal):
    nz = tm_size // NX
    quarter = width // NX
    npix = tm_size * TP
    zpix = NX * TP
    block_rows = rows // nblocks
    shifts = quarter + 2 * SW
    far = nz // 2

    def kernel(
        spec, basis_in, weight, routes, offsets, taps, gal_pix, gal_chan,
        sky, stacked,
        own, basis, pix, raw, gram, proj, ext, coef, band, ripple, clean, part, pixel_hot, counts,
        zsend, zrecv, edge, final, mine, st1, st2, st3,
        load_sem, pix_s, pix_r, raw_s, raw_r, gram_s, gram_r, proj_s, proj_r, coef_s, coef_r,
        z_s, z_r, edge_r, mine_s, mine_r, st1_s, st1_r, st2_s, st2_r, st3_s, st3_r,
    ):
        tm = lax.axis_index("tm")
        j = lax.axis_index("chan")
        z = lax.div(tm, NX)
        x = lax.rem(tm, NX)
        here = pl.multiple_of(x * quarter, quarter)

        def x_peer(r):
            return (z * NX + lax.rem(x + r, NX), j)

        def c_peer(r):
            return (tm, lax.rem(j + r, chan_size))

        def z_peer(r):
            return (lax.rem(z + r, nz) * NX + x, j)

        def beside(way, place):
            return (lax.rem(place[0] + (NX, (nz - 1) * NX)[way], tm_size), place[1])

        def remote(src, dst, send_sem, recv_sem, peer):
            return pltpu.make_async_remote_copy(
                src_ref=src, dst_ref=dst, send_sem=send_sem, recv_sem=recv_sem,
                device_id=peer, device_id_type=MESH,
            )

        sends = []

        def start(copy):
            copy.start()
            sends.append(copy)

        peers = (
            [x_peer(r) for r in range(1, NX)]
            + [c_peer(r) for r in range(1, chan_size)]
            + [z_peer(r) for r in range(1, nz)]
            + [beside(way, x_peer(r)) for way in range(2) for r in range(1, NX)]
        )
        barrier = pltpu.get_barrier_semaphore()
        for peer in peers:
            pl.semaphore_signal(barrier, inc=1, device_id=peer, device_id_type=MESH)
        basis_here = basis_in.at[:, pl.ds(pl.multiple_of(j * width, width), width)]
        loads = [
            pltpu.make_async_copy(source, target, load_sem.at[i])
            for i, (source, target) in enumerate((
                (spec, own), (basis_here, basis),
            ))
        ]
        for load in loads:
            load.start()
        inside = iota((nblocks, rows), 1) - block_rows * iota((nblocks, rows), 0)
        owner = ((inside >= 0) & (inside < block_rows)).astype(f32).astype(bf16)
        tile = jnp.dot(
            jnp.broadcast_to(routes[...], (16, nblocks)).astype(f32).astype(bf16), owner,
            preferred_element_type=f32,
        )[0:1].astype(jnp.int32)
        pix[0] = tile * TP + offsets[...] - MARGIN

        loads[1].wait()
        weighted = basis[...] * weight[...]
        w_stack = jnp.concatenate(split3(weighted), axis=0)

        pl.semaphore_wait(barrier, len(peers))
        for r in range(1, NX):
            start(remote(pix.at[0], pix.at[NX - r], pix_s.at[r], pix_r.at[NX - r], x_peer(r)))

        late = rows // 4 * 3

        def raw_copy(r, piece):
            column = pl.multiple_of(lax.rem(x + r, NX) * quarter, quarter)
            low, high = ((0, late), (late, rows), (0, rows))[piece]
            return remote(
                own.at[low:high, pl.ds(column, quarter)], raw.at[NX - r, low:high],
                raw_s.at[piece, r], raw_r.at[piece, NX - r], x_peer(r),
            )

        loads[0].wait()
        for r, piece in ((2, 2), (1, 0), (3, 0)):
            start(raw_copy(r, piece))

        products = lax.dot_general(
            w_stack, own[...], (((1,), (1,)), ((), ())), preferred_element_type=f32
        )
        proj[0] = products[:MODES] + products[MODES:2 * MODES] + products[2 * MODES:]
        for r in range(1, chan_size):
            start(remote(
                proj.at[0], proj.at[chan_size - r], proj_s.at[r], proj_r.at[chan_size - r],
                c_peer(r),
            ))
        gram[0] = jnp.zeros((MODES, 128), f32)
        gram[0, :, 0:MODES] = lax.dot_general(
            weighted, basis[...], (((1,), (1,)), ((), ())), precision=highest,
            preferred_element_type=f32,
        )
        for r in range(1, chan_size):
            start(remote(
                gram.at[0], gram.at[chan_size - r], gram_s.at[r], gram_r.at[chan_size - r],
                c_peer(r),
            ))

        def fill(target, column, group, tap):
            def step(a, carry):
                row = pl.multiple_of(a * TAPS, TAPS)
                target[pl.ds(row, TAPS), column:column + tap.shape[1]] = jnp.where(
                    group == a, tap, 0.0
                ).astype(bf16)
                return carry

            lax.fori_loop(0, npix // TAPS, step, 0, unroll=4)

        def build_band(slot):
            first = pix[slot]
            group = jnp.broadcast_to(first >> 4, (TAPS, rows))
            inner = jnp.broadcast_to(first & (TAPS - 1), (TAPS, rows))
            lane = iota((TAPS, rows), 0)
            turn = (lane - inner) & (TAPS - 1)
            tap = jnp.zeros((TAPS, rows), f32)
            values = taps[...].astype(f32)
            for m in range(TAPS):
                tap = jnp.where(turn == m, values[0:1, m:m + 1], tap)
            fill(band, slot * rows, jnp.where(lane < inner, group + 1, group), tap)

        build_band(0)

        for r in range(1, chan_size):
            remote(gram.at[0], gram.at[r], gram_s.at[r], gram_r.at[r], c_peer(r)).wait_recv()
        total = gram[0]
        for r in range(1, chan_size):
            total = total + gram[r]
        row_id = iota((MODES, 128), 0)
        both = jnp.where(iota((MODES, 128), 1) - MODES == row_id, 1.0, total)
        for i in range(MODES):
            pivot = both[i:i + 1, :] / both[i:i + 1, i:i + 1]
            both = jnp.where(row_id == i, pivot, both - both[:, i:i + 1] * pivot)

        ext[...] = jnp.zeros(ext.shape, f32)
        for r in range(1, chan_size):
            remote(proj.at[0], proj.at[r], proj_s.at[r], proj_r.at[r], c_peer(r)).wait_recv()
        full = proj[0]
        for r in range(1, chan_size):
            full = full + proj[r]
        ext[MODES:2 * MODES, :] = full
        coef[0] = jnp.dot(both, ext[...], precision=highest, preferred_element_type=f32)
        for r in range(1, NX):
            start(remote(coef.at[0], coef.at[NX - r], coef_s.at[r], coef_r.at[NX - r], x_peer(r)))
        for r in (1, 3):
            start(raw_copy(r, 1))

        b_high, b_mid, b_low = split3(basis[:, pl.ds(here, quarter)])
        b_stack = jnp.concatenate(
            [b_high, b_mid, b_high, b_mid, b_low, b_high, jnp.zeros((2 * MODES, quarter), bf16)],
            axis=0,
        )

        def fit_slot(slot):
            c_high, c_mid, c_low = split3(coef[slot])
            c_stack = jnp.concatenate(
                [c_high, c_high, c_mid, c_mid, c_high, c_low, jnp.zeros((2 * MODES, rows), bf16)],
                axis=0,
            )
            ripple[slot * rows:(slot + 1) * rows, :] = lax.dot_general(
                c_stack, b_stack, (((0,), (0,)), ((), ())), preferred_element_type=f32
            )

        def clean_slot(slot, values):
            clean[slot * rows:(slot + 1) * rows, :] = (
                values.astype(f32) - ripple[slot * rows:(slot + 1) * rows, :]
            ).astype(bf16)

        fit_slot(0)
        clean_slot(0, own[:, pl.ds(here, quarter)])
        begin = gal_chan[...] - SW - (j * width + here)
        shift_hot = (iota((shifts, ngal), 0) == quarter - 1 - begin).astype(f32).astype(bf16)
        gal_row = jnp.broadcast_to(gal_pix[...], (TAPS, ngal))
        fill(
            pixel_hot, 0, gal_row >> 4,
            jnp.where((gal_row & (TAPS - 1)) == iota((TAPS, ngal), 0), 1.0, 0.0).astype(f32),
        )
        counts[...] = lax.dot_general(
            shift_hot, pixel_hot[...], (((1,), (1,)), ((), ())), preferred_element_type=f32
        ).astype(bf16)

        for r in range(1, NX):
            remote(pix.at[0], pix.at[r], pix_s.at[r], pix_r.at[r], x_peer(r)).wait_recv()
            build_band(r)
        for r in (1, 3, 2):
            remote(coef.at[0], coef.at[r], coef_s.at[r], coef_r.at[r], x_peer(r)).wait_recv()
            fit_slot(r)
        for r, pieces in ((2, (2,)), (1, (0, 1)), (3, (0, 1))):
            for piece in pieces:
                raw_copy(NX - r, piece).wait_recv()
            clean_slot(r, raw[r])

        def chunk_row(step):
            return pl.multiple_of(lax.rem(z + step + 2 * nz, nz) * zpix, zpix)

        def part_tile(step, tile):
            row = pl.multiple_of(chunk_row(step) + tile * TP, TP)
            return part[pl.ds(row, TP), :]

        sign = (1, -1)

        def hops(way, tile):
            return far if tile // 2 == way else far - 1

        def z_copy(way, tile, k):
            if k < hops(way, tile) - 1:
                target, recv_sem = zrecv.at[way, tile, k], z_r.at[way, tile, k]
                peer = z_peer((1, nz - 1)[way])
            else:
                target, recv_sem = edge.at[way, x], edge_r.at[way, x]
                peer = beside(way, (z * NX + tile, j))
            return remote(
                zsend.at[way, tile, k], target, z_s.at[way, tile, k], recv_sem, peer
            )

        def z_step(k, long):
            for lane in range(2):
                for way in range(2):
                    tile = 2 * (way if long else 1 - way) + lane
                    value = part_tile(sign[way] * (hops(way, tile) - k), tile)
                    if k:
                        z_copy(way, tile, k - 1).wait_recv()
                        value = value + zrecv[way, tile, k - 1].astype(f32)
                    zsend[way, tile, k] = value.astype(bf16)
                    z_copy(way, tile, k).start()

        def grid_step(n, carry):
            away = lax.div(n + 1, 2)
            row = chunk_row(far + away - 2 * lax.rem(n, 2) * away)
            part[pl.ds(row, zpix), :] = jnp.dot(
                band[pl.ds(row, zpix), :], clean[...], preferred_element_type=f32
            )

            @pl.when(n == 0)
            def _():
                z_step(0, True)

            @pl.when(n == 2)
            def _():
                z_step(0, False)

            @pl.when(n == 4)
            def _():
                z_step(1, True)
                z_step(1, False)

            return carry

        def share(buffer, me, send_sem, recv_sem, peer_of, count):
            for r in range(1, count):
                start(remote(buffer.at[me], buffer.at[me], send_sem.at[r], recv_sem.at[me], peer_of(r)))

        def gather(buffer, me, send_sem, recv_sem, peer_of, count):
            for r in range(1, count):
                other = lax.rem(me + r, count)
                remote(
                    buffer.at[other], buffer.at[other], send_sem.at[r], recv_sem.at[other], peer_of(r)
                ).wait_recv()
            value = buffer[0]
            for i in range(1, count):
                value = value + buffer[i]
            return value

        lax.fori_loop(0, nz, grid_step, 0)

        final[...] = part[pl.ds(chunk_row(0), zpix), :].astype(bf16)
        for r in range(1, NX):
            row = pl.multiple_of(lax.rem(x + r, NX) * TP, TP)
            start(remote(
                final.at[pl.ds(row, TP), :], mine.at[NX - r], mine_s.at[r], mine_r.at[NX - r],
                x_peer(r),
            ))

        wide = jnp.concatenate(
            [
                jnp.dot(counts[...], part[...].astype(bf16), preferred_element_type=f32),
                jnp.zeros((shifts, 512 - quarter), f32),
            ],
            axis=1,
        )
        folded = jnp.zeros((8, 512), f32)
        for i in range(shifts // 8):
            folded = folded + pltpu.roll(
                wide[8 * i:8 * i + 8], (513 - quarter + 8 * i) % 512, 1
            )
        window = jnp.zeros((1, 512), f32)
        for i in range(8):
            window = window + (pltpu.roll(folded[i:i + 1], i, 1) if i else folded[i:i + 1])
        st1[x] = window[:, :2 * SW]
        share(st1, x, st1_s, st1_r, x_peer, NX)

        z_step(2, True)
        st2[j] = gather(st1, x, st1_s, st1_r, x_peer, NX)
        share(st2, j, st2_s, st2_r, c_peer, chan_size)
        z_step(2, False)
        z_step(3, True)
        st3[z] = gather(st2, j, st2_s, st2_r, c_peer, chan_size)
        share(st3, z, st3_s, st3_r, z_peer, nz)
        for r in range(1, NX):
            remote(
                final.at[pl.ds(0, TP), :], mine.at[r], mine_s.at[r], mine_r.at[r], x_peer(r)
            ).wait_recv()
        for copy in sends:
            copy.wait_send()
        for way in range(2):
            for source in range(NX):
                remote(
                    zsend.at[way, 0, 0], edge.at[way, source], z_s.at[way, 0, 0],
                    edge_r.at[way, source], beside(way, x_peer(0)),
                ).wait_recv()
        for r in range(NX):
            source = lax.rem(x + r, NX)
            if r:
                value = mine[r].astype(f32)
            else:
                value = part[pl.ds(pl.multiple_of(chunk_row(0) + x * TP, TP), TP), :]
            value = value + edge[0, source].astype(f32) + edge[1, source].astype(f32)
            column = pl.multiple_of(source * quarter, quarter)
            sky[:, pl.ds(column, quarter)] = value.astype(bf16)
        stacked[...] = gather(st3, z, st3_s, st3_r, z_peer, nz) / ngal
        for way in range(2):
            for tile in range(NX):
                for k in range(hops(way, tile)):
                    z_copy(way, tile, k).wait_send()

    dma = pltpu.SemaphoreType.DMA
    scratch = [
        pltpu.VMEM((rows, width), bf16),
        pltpu.VMEM((MODES, width), f32),
        pltpu.VMEM((NX, 1, rows), jnp.int32),
        pltpu.VMEM((NX, rows, quarter), bf16),
        pltpu.VMEM((chan_size, MODES, 128), f32),
        pltpu.VMEM((chan_size, MODES, rows), f32),
        pltpu.VMEM((128, rows), f32),
        pltpu.VMEM((NX, MODES, rows), f32),
        pltpu.VMEM((npix, NX * rows), bf16),
        pltpu.VMEM((NX * rows, quarter), f32),
        pltpu.VMEM((NX * rows, quarter), bf16),
        pltpu.VMEM((npix, quarter), f32),
        pltpu.VMEM((npix, ngal), bf16),
        pltpu.VMEM((shifts, npix), bf16),
        pltpu.VMEM((2, NX, far, TP, quarter), bf16),
        pltpu.VMEM((2, NX, far - 1, TP, quarter), bf16),
        pltpu.VMEM((2, NX, TP, quarter), bf16),
        pltpu.VMEM((zpix, quarter), bf16),
        pltpu.VMEM((NX, TP, quarter), bf16),
        pltpu.VMEM((NX, 1, 2 * SW), f32),
        pltpu.VMEM((chan_size, 1, 2 * SW), f32),
        pltpu.VMEM((nz, 1, 2 * SW), f32),
        dma((2,)),
    ]
    for shape in ((NX,), (3, NX), (chan_size,), (chan_size,), (NX,)):
        scratch += [dma(shape), dma(shape)]
    scratch += [dma((2, NX, far)), dma((2, NX, far - 1)), dma((2, NX))]
    for shape in ((NX,), (NX,), (chan_size,), (nz,)):
        scratch += [dma(shape), dma(shape)]
    return kernel, scratch


def solution(mesh):
    tm_size, chan_size = mesh.shape["tm"], mesh.shape["chan"]

    def per_device(spectra, chan_weight, routes, offsets, taps, gal_pix, gal_chan):
        rows, width = spectra.shape
        nblocks = routes.shape[0]
        kernel, scratch = make_kernel(
            tm_size, chan_size, rows, width, nblocks, gal_pix.shape[0]
        )
        vmem = pl.BlockSpec(memory_space=pltpu.VMEM)
        sky, stacked = pl.pallas_call(
            kernel,
            out_shape=(
                jax.ShapeDtypeStruct((TP, width), bf16),
                jax.ShapeDtypeStruct((1, 2 * SW), f32),
            ),
            in_specs=[pl.BlockSpec(memory_space=pl.ANY)] * 2 + [vmem] * 6,
            out_specs=(vmem, vmem),
            scratch_shapes=scratch,
            compiler_params=pltpu.CompilerParams(
                collective_id=0, has_side_effects=True, vmem_limit_bytes=54880 * 1024
            ),
        )(
            spectra, jnp.asarray(basis_table(width * chan_size)), chan_weight[None, :],
            routes.reshape(1, nblocks), offsets[None, :], taps[None, :], gal_pix[None, :],
            gal_chan[None, :],
        )
        return sky, stacked[0]

    in_specs = (
        P("tm", "chan"), P("chan"), P("tm", None), P("tm"), P(None), P(None), P(None)
    )
    return jax.shard_map(
        per_device, mesh=mesh, in_specs=in_specs, out_specs=(P("tm", "chan"), P(None)),
        check_vma=False,
    )
```

profile of v0, /device:TPU:1, one launch (start us, length us, event | category | flops | bytes accessed | tf_op | source)
XLA Modules:
  0.0 49.0 jit_solution(18072199120963760839)
XLA Ops:
  0.6 0.0 copy-start.3
  0.6 0.0 copy-start.5
  0.7 0.0 copy-start
  0.7 0.0 copy-start.1
  0.7 0.0 copy-start.2
  0.7 0.0 copy-start.4
  0.7 0.6 %copy-done.3 = s32[256]{0:T(256)S(1)} copy-done((s32[256]{0:T(256)S(1)}, s32[256]{0:T(256)}, u32[]{:S(2)}) %copy-start.3) | copy-done | bytes 1048
  1.3 0.0 copy-done.5
  1.3 0.0 copy-done
  1.4 0.0 copy-done.1
  1.4 0.0 copy-done.2
  1.4 0.0 copy-done.4
  1.4 46.4 %shard_map.95 = (bf16[64,1024]{1,0:T(8,128)(2,1)S(1)}, f32[1,128]{1,0:T(1,128)S(1)}) custom-call(bf16[512,1024]{1,0:T(8,128)(2,1)} %spec.1, f32[16,8192]{1,0:T(8,128)} %constant.2.clone.basis_in, f32[1,1024]{1,0:T(1,128)S(1)} %bitcast.7, s32[1,32]{1,0:T(1,128)S(1)} %bitcast.11, s32[1,512]{1,0:T(1,128)S(1)} %bitcast.8, bf16[1,16]{1,0:T(2,128)(2,1)S(1)} %bitcast.12, ...), custom_call_target="tpu_custom_call" | custom-call | tf_op jit(solution)/shard_map/pallas_call | solution.py:426
  47.8 0.7 %copy.12 = bf16[64,1024]{1,0:T(8,128)(2,1)} copy(bf16[64,1024]{1,0:T(8,128)(2,1)S(1)} %get-tuple-element.8) | data formatting | bytes 262144
  48.5 0.5 %copy.13 = f32[128]{0:T(128)} copy(f32[128]{0:T(128)S(1)} %bitcast.13) | data formatting | bytes 1024
Async XLA Ops:
  0.6 0.7 %copy-start.3 = (s32[256]{0:T(256)S(1)}, s32[256]{0:T(256)}, u32[]{:S(2)}) copy-start(s32[256]{0:T(256)} %param.14) | copy-start | bytes 3076
  0.6 0.7 %copy-start.5 = (bf16[16]{0:T(256)(128)(2,1)S(1)}, bf16[16]{0:T(256)(128)(2,1)}, u32[]{:S(2)}) copy-start(bf16[16]{0:T(256)(128)(2,1)} %param.12) | copy-start | bytes 100
  0.7 0.7 %copy-start = (f32[1024]{0:T(1024)S(1)}, f32[1024]{0:T(1024)}, u32[]{:S(2)}) copy-start(f32[1024]{0:T(1024)} %param.9) | copy-start | bytes 12292
  0.7 0.7 %copy-start.1 = (s32[512]{0:T(512)S(1)}, s32[512]{0:T(512)}, u32[]{:S(2)}) copy-start(s32[512]{0:T(512)} %param.11) | copy-start | bytes 6148
  0.7 0.7 %copy-start.2 = (s32[256]{0:T(256)S(1)}, s32[256]{0:T(256)}, u32[]{:S(2)}) copy-start(s32[256]{0:T(256)} %param.13) | copy-start | bytes 3076
  0.7 0.7 %copy-start.4 = (s32[32,1]{0,1:T(1,128)S(1)}, s32[32,1]{0,1:T(1,128)}, u32[]{:S(2)}) copy-start(s32[32,1]{0,1:T(1,128)} %param.10) | copy-start | bytes 388
where the time goes:
time: 49.1 us; the launch traced here: 49 us
  Pallas kernels  46.4 us (95%)
  local copies, waits for them, and re-layouts  1.86 us (4%)
  between operations  0.69 us (1%)
    pallas_call x1, Pallas kernels, per_device(): pl.pallas_call(kernel, out_shape=(jax.ShapeDtypeStruct((TP, width), bf16)...  46.4 us
    unnamed x14, local copies, waits for them, and re-layouts  1.86 us

commit v1 on v0

--- a/solution.py
+++ b/solution.py
@@ -295,11 +295,6 @@
             def _():
                 z_step(0, False)
 
-            @pl.when(n == 4)
-            def _():
-                z_step(1, True)
-                z_step(1, False)
-
             return carry
 
         def share(buffer, me, send_sem, recv_sem, peer_of, count):
@@ -319,6 +314,26 @@
 
         lax.fori_loop(0, nz, grid_step, 0)
 
+        wide = jnp.concatenate(
+            [
+                jnp.dot(counts[...], part[...].astype(bf16), preferred_element_type=f32),
+                jnp.zeros((shifts, 512 - quarter), f32),
+            ],
+            axis=1,
+        )
+        folded = jnp.zeros((8, 512), f32)
+        for i in range(shifts // 8):
+            folded = folded + pltpu.roll(
+                wide[8 * i:8 * i + 8], (513 - quarter + 8 * i) % 512, 1
+            )
+        window = jnp.zeros((1, 512), f32)
+        for i in range(8):
+            window = window + (pltpu.roll(folded[i:i + 1], i, 1) if i else folded[i:i + 1])
+        st1[x] = window[:, :2 * SW]
+        share(st1, x, st1_s, st1_r, x_peer, NX)
+
+        z_step(1, True)
+        z_step(1, False)
         final[...] = part[pl.ds(chunk_row(0), zpix), :].astype(bf16)
         for r in range(1, NX):
             row = pl.multiple_of(lax.rem(x + r, NX) * TP, TP)
@@ -326,32 +341,13 @@
                 final.at[pl.ds(row, TP), :], mine.at[NX - r], mine_s.at[r], mine_r.at[NX - r],
                 x_peer(r),
             ))
-
-        wide = jnp.concatenate(
-            [
-                jnp.dot(counts[...], part[...].astype(bf16), preferred_element_type=f32),
-                jnp.zeros((shifts, 512 - quarter), f32),
-            ],
-            axis=1,
-        )
-        folded = jnp.zeros((8, 512), f32)
-        for i in range(shifts // 8):
-            folded = folded + pltpu.roll(
-                wide[8 * i:8 * i + 8], (513 - quarter + 8 * i) % 512, 1
-            )
-        window = jnp.zeros((1, 512), f32)
-        for i in range(8):
-            window = window + (pltpu.roll(folded[i:i + 1], i, 1) if i else folded[i:i + 1])
-        st1[x] = window[:, :2 * SW]
-        share(st1, x, st1_s, st1_r, x_peer, NX)
-
-        z_step(2, True)
         st2[j] = gather(st1, x, st1_s, st1_r, x_peer, NX)
         share(st2, j, st2_s, st2_r, c_peer, chan_size)
+        z_step(2, True)
         z_step(2, False)
-        z_step(3, True)
         st3[z] = gather(st2, j, st2_s, st2_r, c_peer, chan_size)
         share(st3, z, st3_s, st3_r, z_peer, nz)
+        z_step(3, True)
         for r in range(1, NX):
             remote(
                 final.at[pl.ds(0, TP), :], mine.at[r], mine_s.at[r], mine_r.at[r], x_peer(r)

time: 49.1 us -> 44.5 us (0.906)
  Pallas kernels: 46.4 us -> 41.8 us
    pallas_call x1, Pallas kernels: 46.4 us -> 41.8 us  [per_device(): pl.pallas_call(kernel, out_shape=(jax.ShapeDtypeStruct((TP, width), bf16)...]
where the time goes in v1:
time: 44.5 us; the launch traced here: 44.4 us
  Pallas kernels  41.8 us (94%)
  local copies, waits for them, and re-layouts  1.86 us (4%)
  between operations  0.69 us (2%)
    pallas_call x1, Pallas kernels, per_device(): pl.pallas_call(kernel, out_shape=(jax.ShapeDtypeStruct((TP, width), bf16)...  41.8 us
    unnamed x14, local copies, waits for them, and re-layouts  1.86 us

profile of v1, /device:TPU:1, one launch (start us, length us, event | category | flops | bytes accessed | tf_op | source)
XLA Modules:
  0.0 44.4 jit_solution(13188481041743130596)
XLA Ops:
  0.6 0.0 copy-start.3
  0.6 0.0 copy-start.5
  0.7 0.0 copy-start
  0.7 0.0 copy-start.1
  0.7 0.0 copy-start.2
  0.7 0.0 copy-start.4
  0.7 0.6 %copy-done.3 = s32[256]{0:T(256)S(1)} copy-done((s32[256]{0:T(256)S(1)}, s32[256]{0:T(256)}, u32[]{:S(2)}) %copy-start.3) | copy-done | bytes 1048
  1.3 0.0 copy-done.5
  1.3 0.0 copy-done
  1.4 0.0 copy-done.1
  1.4 0.0 copy-done.2
  1.4 0.0 copy-done.4
  1.4 41.8 %shard_map.95 = (bf16[64,1024]{1,0:T(8,128)(2,1)S(1)}, f32[1,128]{1,0:T(1,128)S(1)}) custom-call(bf16[512,1024]{1,0:T(8,128)(2,1)} %spec.1, f32[16,8192]{1,0:T(8,128)} %constant.2.clone.basis_in, f32[1,1024]{1,0:T(1,128)S(1)} %bitcast.7, s32[1,32]{1,0:T(1,128)S(1)} %bitcast.11, s32[1,512]{1,0:T(1,128)S(1)} %bitcast.8, bf16[1,16]{1,0:T(2,128)(2,1)S(1)} %bitcast.12, ...), custom_call_target="tpu_custom_call" | custom-call | tf_op jit(solution)/shard_map/pallas_call | solution.py:422
  43.2 0.7 %copy.12 = bf16[64,1024]{1,0:T(8,128)(2,1)} copy(bf16[64,1024]{1,0:T(8,128)(2,1)S(1)} %get-tuple-element.8) | data formatting | bytes 262144
  43.9 0.5 %copy.13 = f32[128]{0:T(128)} copy(f32[128]{0:T(128)S(1)} %bitcast.13) | data formatting | bytes 1024
Async XLA Ops:
  0.6 0.7 %copy-start.3 = (s32[256]{0:T(256)S(1)}, s32[256]{0:T(256)}, u32[]{:S(2)}) copy-start(s32[256]{0:T(256)} %param.14) | copy-start | bytes 3076
  0.6 0.7 %copy-start.5 = (bf16[16]{0:T(256)(128)(2,1)S(1)}, bf16[16]{0:T(256)(128)(2,1)}, u32[]{:S(2)}) copy-start(bf16[16]{0:T(256)(128)(2,1)} %param.12) | copy-start | bytes 100
  0.7 0.7 %copy-start = (f32[1024]{0:T(1024)S(1)}, f32[1024]{0:T(1024)}, u32[]{:S(2)}) copy-start(f32[1024]{0:T(1024)} %param.9) | copy-start | bytes 12292
  0.7 0.7 %copy-start.1 = (s32[512]{0:T(512)S(1)}, s32[512]{0:T(512)}, u32[]{:S(2)}) copy-start(s32[512]{0:T(512)} %param.11) | copy-start | bytes 6148
  0.7 0.7 %copy-start.2 = (s32[256]{0:T(256)S(1)}, s32[256]{0:T(256)}, u32[]{:S(2)}) copy-start(s32[256]{0:T(256)} %param.13) | copy-start | bytes 3076
  0.7 0.7 %copy-start.4 = (s32[32,1]{0,1:T(1,128)S(1)}, s32[32,1]{0,1:T(1,128)}, u32[]{:S(2)}) copy-start(s32[32,1]{0,1:T(1,128)} %param.10) | copy-start | bytes 388

commit v2 on v1

--- a/solution.py
+++ b/solution.py
@@ -111,10 +111,6 @@
         )[0:1].astype(jnp.int32)
         pix[0] = tile * TP + offsets[...] - MARGIN
 
-        loads[1].wait()
-        weighted = basis[...] * weight[...]
-        w_stack = jnp.concatenate(split3(weighted), axis=0)
-
         pl.semaphore_wait(barrier, len(peers))
         for r in range(1, NX):
             start(remote(pix.at[0], pix.at[NX - r], pix_s.at[r], pix_r.at[NX - r], x_peer(r)))
@@ -125,14 +121,17 @@
             column = pl.multiple_of(lax.rem(x + r, NX) * quarter, quarter)
             low, high = ((0, late), (late, rows), (0, rows))[piece]
             return remote(
-                own.at[low:high, pl.ds(column, quarter)], raw.at[NX - r, low:high],
+                spec.at[low:high, pl.ds(column, quarter)], raw.at[NX - r, low:high],
                 raw_s.at[piece, r], raw_r.at[piece, NX - r], x_peer(r),
             )
 
-        loads[0].wait()
         for r, piece in ((2, 2), (1, 0), (3, 0)):
             start(raw_copy(r, piece))
 
+        loads[1].wait()
+        weighted = basis[...] * weight[...]
+        w_stack = jnp.concatenate(split3(weighted), axis=0)
+        loads[0].wait()
         products = lax.dot_general(
             w_stack, own[...], (((1,), (1,)), ((), ())), preferred_element_type=f32
         )
@@ -279,6 +278,13 @@
                         value = value + zrecv[way, tile, k - 1].astype(f32)
                     zsend[way, tile, k] = value.astype(bf16)
                     z_copy(way, tile, k).start()
+
+        def z_sent(last):
+            for way in range(2):
+                for tile in range(NX):
+                    count = hops(way, tile)
+                    for k in (count - 1,) if last else range(count - 1):
+                        z_copy(way, tile, k).wait_send()
 
         def grid_step(n, carry):
             away = lax.div(n + 1, 2)
@@ -354,6 +360,8 @@
             ).wait_recv()
         for copy in sends:
             copy.wait_send()
+        z_sent(False)
+
         for way in range(2):
             for source in range(NX):
                 remote(
@@ -370,10 +378,7 @@
             column = pl.multiple_of(source * quarter, quarter)
             sky[:, pl.ds(column, quarter)] = value.astype(bf16)
         stacked[...] = gather(st3, z, st3_s, st3_r, z_peer, nz) / ngal
-        for way in range(2):
-            for tile in range(NX):
-                for k in range(hops(way, tile)):
-                    z_copy(way, tile, k).wait_send()
+        z_sent(True)
 
     dma = pltpu.SemaphoreType.DMA
     scratch = [

time: 44.5 us -> 44.6 us (level)
  no operation moved by 1% of the time
where the time goes in v2:
time: 44.6 us; the launch traced here: 44.5 us
  Pallas kernels  41.9 us (94%)
  local copies, waits for them, and re-layouts  1.86 us (4%)
  between operations  0.69 us (2%)
    pallas_call x1, Pallas kernels, per_device(): pl.pallas_call(kernel, out_shape=(jax.ShapeDtypeStruct((TP, width), bf16)...  41.9 us
    unnamed x14, local copies, waits for them, and re-layouts  1.86 us

profile of v2, /device:TPU:1, one launch (start us, length us, event | category | flops | bytes accessed | tf_op | source)
XLA Modules:
  0.0 44.5 jit_solution(16787930054466329089)
XLA Ops:
  0.6 0.0 copy-start.3
  0.6 0.0 copy-start.5
  0.7 0.0 copy-start
  0.7 0.0 copy-start.1
  0.7 0.0 copy-start.2
  0.7 0.0 copy-start.4
  0.7 0.6 %copy-done.3 = s32[256]{0:T(256)S(1)} copy-done((s32[256]{0:T(256)S(1)}, s32[256]{0:T(256)}, u32[]{:S(2)}) %copy-start.3) | copy-done | bytes 1048
  1.3 0.0 copy-done.5
  1.3 0.0 copy-done
  1.4 0.0 copy-done.1
  1.4 0.0 copy-done.2
  1.4 0.0 copy-done.4
  1.4 41.9 %shard_map.95 = (bf16[64,1024]{1,0:T(8,128)(2,1)S(1)}, f32[1,128]{1,0:T(1,128)S(1)}) custom-call(bf16[512,1024]{1,0:T(8,128)(2,1)} %spec.1, f32[16,8192]{1,0:T(8,128)} %constant.2.clone.basis_in, f32[1,1024]{1,0:T(1,128)S(1)} %bitcast.7, s32[1,32]{1,0:T(1,128)S(1)} %bitcast.11, s32[1,512]{1,0:T(1,128)S(1)} %bitcast.8, bf16[1,16]{1,0:T(2,128)(2,1)S(1)} %bitcast.12, ...), custom_call_target="tpu_custom_call" | custom-call | tf_op jit(solution)/shard_map/pallas_call | solution.py:427
  43.3 0.7 %copy.12 = bf16[64,1024]{1,0:T(8,128)(2,1)} copy(bf16[64,1024]{1,0:T(8,128)(2,1)S(1)} %get-tuple-element.8) | data formatting | bytes 262144
  44.0 0.5 %copy.13 = f32[128]{0:T(128)} copy(f32[128]{0:T(128)S(1)} %bitcast.13) | data formatting | bytes 1024
Async XLA Ops:
  0.6 0.7 %copy-start.3 = (s32[256]{0:T(256)S(1)}, s32[256]{0:T(256)}, u32[]{:S(2)}) copy-start(s32[256]{0:T(256)} %param.14) | copy-start | bytes 3076
  0.6 0.7 %copy-start.5 = (bf16[16]{0:T(256)(128)(2,1)S(1)}, bf16[16]{0:T(256)(128)(2,1)}, u32[]{:S(2)}) copy-start(bf16[16]{0:T(256)(128)(2,1)} %param.12) | copy-start | bytes 100
  0.7 0.7 %copy-start = (f32[1024]{0:T(1024)S(1)}, f32[1024]{0:T(1024)}, u32[]{:S(2)}) copy-start(f32[1024]{0:T(1024)} %param.9) | copy-start | bytes 12292
  0.7 0.7 %copy-start.1 = (s32[512]{0:T(512)S(1)}, s32[512]{0:T(512)}, u32[]{:S(2)}) copy-start(s32[512]{0:T(512)} %param.11) | copy-start | bytes 6148
  0.7 0.7 %copy-start.2 = (s32[256]{0:T(256)S(1)}, s32[256]{0:T(256)}, u32[]{:S(2)}) copy-start(s32[256]{0:T(256)} %param.13) | copy-start | bytes 3076
  0.7 0.7 %copy-start.4 = (s32[32,1]{0,1:T(1,128)S(1)}, s32[32,1]{0,1:T(1,128)}, u32[]{:S(2)}) copy-start(s32[32,1]{0,1:T(1,128)} %param.10) | copy-start | bytes 388

commit v3 on v2

--- a/solution.py
+++ b/solution.py
@@ -50,7 +50,7 @@
     def kernel(
         spec, basis_in, weight, routes, offsets, taps, gal_pix, gal_chan,
         sky, stacked,
-        own, basis, pix, raw, gram, proj, ext, coef, band, ripple, clean, part, pixel_hot, counts,
+        own, basis, pix, raw, gram, proj, ext, coef, band, clean, part, pixel_hot, counts,
         zsend, zrecv, edge, final, mine, st1, st2, st3,
         load_sem, pix_s, pix_r, raw_s, raw_r, gram_s, gram_r, proj_s, proj_r, coef_s, coef_r,
         z_s, z_r, edge_r, mine_s, mine_r, st1_s, st1_r, st2_s, st2_r, st3_s, st3_r,
@@ -98,7 +98,7 @@
         loads = [
             pltpu.make_async_copy(source, target, load_sem.at[i])
             for i, (source, target) in enumerate((
-                (spec, own), (basis_here, basis),
+                (spec, own.at[0:rows]), (basis_here, basis),
             ))
         ]
         for load in loads:
@@ -131,24 +131,28 @@
         loads[1].wait()
         weighted = basis[...] * weight[...]
         w_stack = jnp.concatenate(split3(weighted), axis=0)
+        own[rows:, :] = jnp.concatenate(
+            [*split3(basis[...]), jnp.zeros((128 - 3 * MODES, width), bf16)], axis=0
+        )
         loads[0].wait()
         products = lax.dot_general(
             w_stack, own[...], (((1,), (1,)), ((), ())), preferred_element_type=f32
         )
-        proj[0] = products[:MODES] + products[MODES:2 * MODES] + products[2 * MODES:]
+        products = products[:MODES] + products[MODES:2 * MODES] + products[2 * MODES:]
+        normal = products[:, rows:]
+        normal = (
+            normal + pltpu.roll(normal, 128 - MODES, 1) + pltpu.roll(normal, 128 - 2 * MODES, 1)
+        )
+        gram[0] = jnp.where(iota((MODES, 128), 1) < MODES, normal, 0.0)
+        for r in range(1, chan_size):
+            start(remote(
+                gram.at[0], gram.at[chan_size - r], gram_s.at[r], gram_r.at[chan_size - r],
+                c_peer(r),
+            ))
+        proj[0] = products[:, :rows]
         for r in range(1, chan_size):
             start(remote(
                 proj.at[0], proj.at[chan_size - r], proj_s.at[r], proj_r.at[chan_size - r],
-                c_peer(r),
-            ))
-        gram[0] = jnp.zeros((MODES, 128), f32)
-        gram[0, :, 0:MODES] = lax.dot_general(
-            weighted, basis[...], (((1,), (1,)), ((), ())), precision=highest,
-            preferred_element_type=f32,
-        )
-        for r in range(1, chan_size):
-            start(remote(
-                gram.at[0], gram.at[chan_size - r], gram_s.at[r], gram_r.at[chan_size - r],
                 c_peer(r),
             ))
 
@@ -206,23 +210,19 @@
             axis=0,
         )
 
-        def fit_slot(slot):
+        def clean_slot(slot, values):
             c_high, c_mid, c_low = split3(coef[slot])
             c_stack = jnp.concatenate(
                 [c_high, c_high, c_mid, c_mid, c_high, c_low, jnp.zeros((2 * MODES, rows), bf16)],
                 axis=0,
             )
-            ripple[slot * rows:(slot + 1) * rows, :] = lax.dot_general(
+            ripple = lax.dot_general(
                 c_stack, b_stack, (((0,), (0,)), ((), ())), preferred_element_type=f32
             )
-
-        def clean_slot(slot, values):
-            clean[slot * rows:(slot + 1) * rows, :] = (
-                values.astype(f32) - ripple[slot * rows:(slot + 1) * rows, :]
-            ).astype(bf16)
-
-        fit_slot(0)
-        clean_slot(0, own[:, pl.ds(here, quarter)])
+            clean[slot * rows:(slot + 1) * rows, :] = (values.astype(f32) - ripple).astype(bf16)
+
+        clean_slot(0, own[0:rows, pl.ds(here, quarter)])
+
         begin = gal_chan[...] - SW - (j * width + here)
         shift_hot = (iota((shifts, ngal), 0) == quarter - 1 - begin).astype(f32).astype(bf16)
         gal_row = jnp.broadcast_to(gal_pix[...], (TAPS, ngal))
@@ -237,12 +237,10 @@
         for r in range(1, NX):
             remote(pix.at[0], pix.at[r], pix_s.at[r], pix_r.at[r], x_peer(r)).wait_recv()
             build_band(r)
-        for r in (1, 3, 2):
-            remote(coef.at[0], coef.at[r], coef_s.at[r], coef_r.at[r], x_peer(r)).wait_recv()
-            fit_slot(r)
-        for r, pieces in ((2, (2,)), (1, (0, 1)), (3, (0, 1))):
+        for r, pieces in ((1, (0, 1)), (3, (0, 1)), (2, (2,))):
             for piece in pieces:
                 raw_copy(NX - r, piece).wait_recv()
+            remote(coef.at[0], coef.at[r], coef_s.at[r], coef_r.at[r], x_peer(r)).wait_recv()
             clean_slot(r, raw[r])
 
         def chunk_row(step):
@@ -382,7 +380,7 @@
 
     dma = pltpu.SemaphoreType.DMA
     scratch = [
-        pltpu.VMEM((rows, width), bf16),
+        pltpu.VMEM((rows + 128, width), bf16),
         pltpu.VMEM((MODES, width), f32),
         pltpu.VMEM((NX, 1, rows), jnp.int32),
         pltpu.VMEM((NX, rows, quarter), bf16),
@@ -391,7 +389,6 @@
         pltpu.VMEM((128, rows), f32),
         pltpu.VMEM((NX, MODES, rows), f32),
         pltpu.VMEM((npix, NX * rows), bf16),
-        pltpu.VMEM((NX * rows, quarter), f32),
         pltpu.VMEM((NX * rows, quarter), bf16),
         pltpu.VMEM((npix, quarter), f32),
         pltpu.VMEM((npix, ngal), bf16),

time: 44.6 us -> 45.2 us (1.013)
  Pallas kernels: 41.9 us -> 42.6 us
    pallas_call x1, Pallas kernels: 41.9 us -> 42.6 us  [per_device(): pl.pallas_call(kernel, out_shape=(jax.ShapeDtypeStruct((TP, width), bf16)...]
where the time goes in v3:
time: 45.2 us; the launch traced here: 45.1 us
  Pallas kernels  42.6 us (94%)
  local copies, waits for them, and re-layouts  1.86 us (4%)
  between operations  0.69 us (2%)
    pallas_call x1, Pallas kernels, per_device(): pl.pallas_call(kernel, out_shape=(jax.ShapeDtypeStruct((TP, width), bf16)...  42.6 us
    unnamed x14, local copies, waits for them, and re-layouts  1.86 us

profile of v3, /device:TPU:1, one launch (start us, length us, event | category | flops | bytes accessed | tf_op | source)
XLA Modules:
  0.0 45.1 jit_solution(613770490789674568)
XLA Ops:
  0.6 0.0 copy-start.3
  0.6 0.0 copy-start.5
  0.7 0.0 copy-start
  0.7 0.0 copy-start.1
  0.7 0.0 copy-start.2
  0.7 0.0 copy-start.4
  0.7 0.6 %copy-done.3 = s32[256]{0:T(256)S(1)} copy-done((s32[256]{0:T(256)S(1)}, s32[256]{0:T(256)}, u32[]{:S(2)}) %copy-start.3) | copy-done | bytes 1048
  1.3 0.0 copy-done.5
  1.3 0.0 copy-done
  1.4 0.0 copy-done.1
  1.4 0.0 copy-done.2
  1.4 0.0 copy-done.4
  1.4 42.6 %shard_map.95 = (bf16[64,1024]{1,0:T(8,128)(2,1)S(1)}, f32[1,128]{1,0:T(1,128)S(1)}) custom-call(bf16[512,1024]{1,0:T(8,128)(2,1)} %spec.1, f32[16,8192]{1,0:T(8,128)} %constant.2.clone.basis_in, f32[1,1024]{1,0:T(1,128)S(1)} %bitcast.7, s32[1,32]{1,0:T(1,128)S(1)} %bitcast.11, s32[1,512]{1,0:T(1,128)S(1)} %bitcast.8, bf16[1,16]{1,0:T(2,128)(2,1)S(1)} %bitcast.12, ...), custom_call_target="tpu_custom_call" | custom-call | tf_op jit(solution)/shard_map/pallas_call | solution.py:424
  44.0 0.7 %copy.12 = bf16[64,1024]{1,0:T(8,128)(2,1)} copy(bf16[64,1024]{1,0:T(8,128)(2,1)S(1)} %get-tuple-element.8) | data formatting | bytes 262144
  44.6 0.5 %copy.13 = f32[128]{0:T(128)} copy(f32[128]{0:T(128)S(1)} %bitcast.13) | data formatting | bytes 1024
Async XLA Ops:
  0.6 0.7 %copy-start.3 = (s32[256]{0:T(256)S(1)}, s32[256]{0:T(256)}, u32[]{:S(2)}) copy-start(s32[256]{0:T(256)} %param.14) | copy-start | bytes 3076
  0.6 0.7 %copy-start.5 = (bf16[16]{0:T(256)(128)(2,1)S(1)}, bf16[16]{0:T(256)(128)(2,1)}, u32[]{:S(2)}) copy-start(bf16[16]{0:T(256)(128)(2,1)} %param.12) | copy-start | bytes 100
  0.7 0.7 %copy-start = (f32[1024]{0:T(1024)S(1)}, f32[1024]{0:T(1024)}, u32[]{:S(2)}) copy-start(f32[1024]{0:T(1024)} %param.9) | copy-start | bytes 12292
  0.7 0.7 %copy-start.1 = (s32[512]{0:T(512)S(1)}, s32[512]{0:T(512)}, u32[]{:S(2)}) copy-start(s32[512]{0:T(512)} %param.11) | copy-start | bytes 6148
  0.7 0.7 %copy-start.2 = (s32[256]{0:T(256)S(1)}, s32[256]{0:T(256)}, u32[]{:S(2)}) copy-start(s32[256]{0:T(256)} %param.13) | copy-start | bytes 3076
  0.7 0.7 %copy-start.4 = (s32[32,1]{0,1:T(1,128)S(1)}, s32[32,1]{0,1:T(1,128)}, u32[]{:S(2)}) copy-start(s32[32,1]{0,1:T(1,128)} %param.10) | copy-start | bytes 388

commit v4 on v3

--- a/solution.py
+++ b/solution.py
@@ -50,7 +50,7 @@
     def kernel(
         spec, basis_in, weight, routes, offsets, taps, gal_pix, gal_chan,
         sky, stacked,
-        own, basis, pix, raw, gram, proj, ext, coef, band, clean, part, pixel_hot, counts,
+        own, basis, pix, raw, gram, proj, ext, coef, band, ripple, clean, part, pixel_hot, counts,
         zsend, zrecv, edge, final, mine, st1, st2, st3,
         load_sem, pix_s, pix_r, raw_s, raw_r, gram_s, gram_r, proj_s, proj_r, coef_s, coef_r,
         z_s, z_r, edge_r, mine_s, mine_r, st1_s, st1_r, st2_s, st2_r, st3_s, st3_r,
@@ -115,18 +115,15 @@
         for r in range(1, NX):
             start(remote(pix.at[0], pix.at[NX - r], pix_s.at[r], pix_r.at[NX - r], x_peer(r)))
 
-        late = rows // 4 * 3
-
-        def raw_copy(r, piece):
+        def raw_copy(r):
             column = pl.multiple_of(lax.rem(x + r, NX) * quarter, quarter)
-            low, high = ((0, late), (late, rows), (0, rows))[piece]
             return remote(
-                spec.at[low:high, pl.ds(column, quarter)], raw.at[NX - r, low:high],
-                raw_s.at[piece, r], raw_r.at[piece, NX - r], x_peer(r),
-            )
-
-        for r, piece in ((2, 2), (1, 0), (3, 0)):
-            start(raw_copy(r, piece))
+                spec.at[:, pl.ds(column, quarter)], raw.at[NX - r], raw_s.at[r], raw_r.at[NX - r],
+                x_peer(r),
+            )
+
+        for r in (2, 1, 3):
+            start(raw_copy(r))
 
         loads[1].wait()
         weighted = basis[...] * weight[...]
@@ -201,8 +198,6 @@
         coef[0] = jnp.dot(both, ext[...], precision=highest, preferred_element_type=f32)
         for r in range(1, NX):
             start(remote(coef.at[0], coef.at[NX - r], coef_s.at[r], coef_r.at[NX - r], x_peer(r)))
-        for r in (1, 3):
-            start(raw_copy(r, 1))
 
         b_high, b_mid, b_low = split3(basis[:, pl.ds(here, quarter)])
         b_stack = jnp.concatenate(
@@ -210,17 +205,22 @@
             axis=0,
         )
 
-        def clean_slot(slot, values):
+        def fit_slot(slot):
             c_high, c_mid, c_low = split3(coef[slot])
             c_stack = jnp.concatenate(
                 [c_high, c_high, c_mid, c_mid, c_high, c_low, jnp.zeros((2 * MODES, rows), bf16)],
                 axis=0,
             )
-            ripple = lax.dot_general(
+            ripple[slot * rows:(slot + 1) * rows, :] = lax.dot_general(
                 c_stack, b_stack, (((0,), (0,)), ((), ())), preferred_element_type=f32
             )
-            clean[slot * rows:(slot + 1) * rows, :] = (values.astype(f32) - ripple).astype(bf16)
-
+
+        def clean_slot(slot, values):
+            clean[slot * rows:(slot + 1) * rows, :] = (
+                values.astype(f32) - ripple[slot * rows:(slot + 1) * rows, :]
+            ).astype(bf16)
+
+        fit_slot(0)
         clean_slot(0, own[0:rows, pl.ds(here, quarter)])
 
         begin = gal_chan[...] - SW - (j * width + here)
@@ -237,10 +237,11 @@
         for r in range(1, NX):
             remote(pix.at[0], pix.at[r], pix_s.at[r], pix_r.at[r], x_peer(r)).wait_recv()
             build_band(r)
-        for r, pieces in ((1, (0, 1)), (3, (0, 1)), (2, (2,))):
-            for piece in pieces:
-                raw_copy(NX - r, piece).wait_recv()
+        for r in (1, 3, 2):
             remote(coef.at[0], coef.at[r], coef_s.at[r], coef_r.at[r], x_peer(r)).wait_recv()
+            fit_slot(r)
+        for r in (1, 3, 2):
+            raw_copy(NX - r).wait_recv()
             clean_slot(r, raw[r])
 
         def chunk_row(step):
@@ -389,6 +390,7 @@
         pltpu.VMEM((128, rows), f32),
         pltpu.VMEM((NX, MODES, rows), f32),
         pltpu.VMEM((npix, NX * rows), bf16),
+        pltpu.VMEM((NX * rows, quarter), f32),
         pltpu.VMEM((NX * rows, quarter), bf16),
         pltpu.VMEM((npix, quarter), f32),
         pltpu.VMEM((npix, ngal), bf16),
@@ -403,7 +405,7 @@
         pltpu.VMEM((nz, 1, 2 * SW), f32),
         dma((2,)),
     ]
-    for shape in ((NX,), (3, NX), (chan_size,), (chan_size,), (NX,)):
+    for shape in ((NX,), (NX,), (chan_size,), (chan_size,), (NX,)):
         scratch += [dma(shape), dma(shape)]
     scratch += [dma((2, NX, far)), dma((2, NX, far - 1)), dma((2, NX))]
     for shape in ((NX,), (NX,), (chan_size,), (nz,)):

time: 45.2 us -> 45.3 us (level)
  no operation moved by 1% of the time
where the time goes in v4:
time: 45.3 us; the launch traced here: 45.2 us
  Pallas kernels  42.6 us (94%)
  local copies, waits for them, and re-layouts  1.86 us (4%)
  between operations  0.69 us (2%)
    pallas_call x1, Pallas kernels, per_device(): pl.pallas_call(kernel, out_shape=(jax.ShapeDtypeStruct((TP, width), bf16)...  42.6 us
    unnamed x14, local copies, waits for them, and re-layouts  1.86 us

profile of v4, /device:TPU:1, one launch (start us, length us, event | category | flops | bytes accessed | tf_op | source)
XLA Modules:
  0.0 45.2 jit_solution(10960320264794793532)
XLA Ops:
  0.6 0.0 copy-start.3
  0.6 0.0 copy-start.5
  0.7 0.0 copy-start
  0.7 0.0 copy-start.1
  0.7 0.0 copy-start.2
  0.7 0.0 copy-start.4
  0.7 0.6 %copy-done.3 = s32[256]{0:T(256)S(1)} copy-done((s32[256]{0:T(256)S(1)}, s32[256]{0:T(256)}, u32[]{:S(2)}) %copy-start.3) | copy-done | bytes 1048
  1.3 0.0 copy-done.5
  1.3 0.0 copy-done
  1.4 0.0 copy-done.1
  1.4 0.0 copy-done.2
  1.4 0.0 copy-done.4
  1.4 42.6 %shard_map.95 = (bf16[64,1024]{1,0:T(8,128)(2,1)S(1)}, f32[1,128]{1,0:T(1,128)S(1)}) custom-call(bf16[512,1024]{1,0:T(8,128)(2,1)} %spec.1, f32[16,8192]{1,0:T(8,128)} %constant.2.clone.basis_in, f32[1,1024]{1,0:T(1,128)S(1)} %bitcast.7, s32[1,32]{1,0:T(1,128)S(1)} %bitcast.11, s32[1,512]{1,0:T(1,128)S(1)} %bitcast.8, bf16[1,16]{1,0:T(2,128)(2,1)S(1)} %bitcast.12, ...), custom_call_target="tpu_custom_call" | custom-call | tf_op jit(solution)/shard_map/pallas_call | solution.py:426
  44.0 0.7 %copy.12 = bf16[64,1024]{1,0:T(8,128)(2,1)} copy(bf16[64,1024]{1,0:T(8,128)(2,1)S(1)} %get-tuple-element.8) | data formatting | bytes 262144
  44.6 0.5 %copy.13 = f32[128]{0:T(128)} copy(f32[128]{0:T(128)S(1)} %bitcast.13) | data formatting | bytes 1024
Async XLA Ops:
  0.6 0.7 %copy-start.3 = (s32[256]{0:T(256)S(1)}, s32[256]{0:T(256)}, u32[]{:S(2)}) copy-start(s32[256]{0:T(256)} %param.14) | copy-start | bytes 3076
  0.6 0.7 %copy-start.5 = (bf16[16]{0:T(256)(128)(2,1)S(1)}, bf16[16]{0:T(256)(128)(2,1)}, u32[]{:S(2)}) copy-start(bf16[16]{0:T(256)(128)(2,1)} %param.12) | copy-start | bytes 100
  0.7 0.7 %copy-start = (f32[1024]{0:T(1024)S(1)}, f32[1024]{0:T(1024)}, u32[]{:S(2)}) copy-start(f32[1024]{0:T(1024)} %param.9) | copy-start | bytes 12292
  0.7 0.7 %copy-start.1 = (s32[512]{0:T(512)S(1)}, s32[512]{0:T(512)}, u32[]{:S(2)}) copy-start(s32[512]{0:T(512)} %param.11) | copy-start | bytes 6148
  0.7 0.7 %copy-start.2 = (s32[256]{0:T(256)S(1)}, s32[256]{0:T(256)}, u32[]{:S(2)}) copy-start(s32[256]{0:T(256)} %param.13) | copy-start | bytes 3076
  0.7 0.7 %copy-start.4 = (s32[32,1]{0,1:T(1,128)S(1)}, s32[32,1]{0,1:T(1,128)}, u32[]{:S(2)}) copy-start(s32[32,1]{0,1:T(1,128)} %param.10) | copy-start | bytes 388

commit v5 on v1

--- a/solution.py
+++ b/solution.py
@@ -70,8 +70,8 @@
         def z_peer(r):
             return (lax.rem(z + r, nz) * NX + x, j)
 
-        def beside(way, place):
-            return (lax.rem(place[0] + (NX, (nz - 1) * NX)[way], tm_size), place[1])
+        def beside(way, place, away):
+            return (lax.rem(place[0] + (away, nz - away)[way] * NX, tm_size), place[1])
 
         def remote(src, dst, send_sem, recv_sem, peer):
             return pltpu.make_async_remote_copy(
@@ -89,7 +89,10 @@
             [x_peer(r) for r in range(1, NX)]
             + [c_peer(r) for r in range(1, chan_size)]
             + [z_peer(r) for r in range(1, nz)]
-            + [beside(way, x_peer(r)) for way in range(2) for r in range(1, NX)]
+            + [
+                beside(way, x_peer(r), away)
+                for away in (1, 2) for way in range(2) for r in range(1, NX)
+            ]
         )
         barrier = pltpu.get_barrier_semaphore()
         for peer in peers:
@@ -255,16 +258,21 @@
 
         sign = (1, -1)
 
-        def hops(way, tile):
-            return far if tile // 2 == way else far - 1
+        def distance(way, tile, k):
+            long = tile // 2 == way
+            return (far, far - 1, far - 2, 1)[k] if long else (far - 1, far - 2, 1)[k]
+
+        def steps(way, tile):
+            return 4 if tile // 2 == way else 3
 
         def z_copy(way, tile, k):
-            if k < hops(way, tile) - 1:
+            if k < 2:
                 target, recv_sem = zrecv.at[way, tile, k], z_r.at[way, tile, k]
                 peer = z_peer((1, nz - 1)[way])
             else:
-                target, recv_sem = edge.at[way, x], edge_r.at[way, x]
-                peer = beside(way, (z * NX + tile, j))
+                slot = way if k == 2 else 2
+                target, recv_sem = edge.at[slot, x], edge_r.at[slot, x]
+                peer = beside(way, (z * NX + tile, j), distance(way, tile, k))
             return remote(
                 zsend.at[way, tile, k], target, z_s.at[way, tile, k], recv_sem, peer
             )
@@ -273,12 +281,19 @@
             for lane in range(2):
                 for way in range(2):
                     tile = 2 * (way if long else 1 - way) + lane
-                    value = part_tile(sign[way] * (hops(way, tile) - k), tile)
-                    if k:
+                    value = part_tile(sign[way] * distance(way, tile, k), tile)
+                    if k in (1, 2):
                         z_copy(way, tile, k - 1).wait_recv()
                         value = value + zrecv[way, tile, k - 1].astype(f32)
                     zsend[way, tile, k] = value.astype(bf16)
                     z_copy(way, tile, k).start()
+
+        def z_sent(ks):
+            for way in range(2):
+                for tile in range(NX):
+                    for k in ks:
+                        if k < steps(way, tile):
+                            z_copy(way, tile, k).wait_send()
 
         def grid_step(n, carry):
             away = lax.div(n + 1, 2)
@@ -345,20 +360,22 @@
         share(st2, j, st2_s, st2_r, c_peer, chan_size)
         z_step(2, True)
         z_step(2, False)
+        z_step(3, True)
         st3[z] = gather(st2, j, st2_s, st2_r, c_peer, chan_size)
         share(st3, z, st3_s, st3_r, z_peer, nz)
-        z_step(3, True)
         for r in range(1, NX):
             remote(
                 final.at[pl.ds(0, TP), :], mine.at[r], mine_s.at[r], mine_r.at[r], x_peer(r)
             ).wait_recv()
         for copy in sends:
             copy.wait_send()
-        for way in range(2):
+        z_sent((0, 1))
+
+        for slot in range(3):
             for source in range(NX):
                 remote(
-                    zsend.at[way, 0, 0], edge.at[way, source], z_s.at[way, 0, 0],
-                    edge_r.at[way, source], beside(way, x_peer(0)),
+                    zsend.at[0, 0, 0], edge.at[slot, source], z_s.at[0, 0, 0],
+                    edge_r.at[slot, source], beside(0, x_peer(0), 1),
                 ).wait_recv()
         for r in range(NX):
             source = lax.rem(x + r, NX)
@@ -366,14 +383,12 @@
                 value = mine[r].astype(f32)
             else:
                 value = part[pl.ds(pl.multiple_of(chunk_row(0) + x * TP, TP), TP), :]
-            value = value + edge[0, source].astype(f32) + edge[1, source].astype(f32)
+            for slot in range(3):
+                value = value + edge[slot, source].astype(f32)
             column = pl.multiple_of(source * quarter, quarter)
             sky[:, pl.ds(column, quarter)] = value.astype(bf16)
         stacked[...] = gather(st3, z, st3_s, st3_r, z_peer, nz) / ngal
-        for way in range(2):
-            for tile in range(NX):
-                for k in range(hops(way, tile)):
-                    z_copy(way, tile, k).wait_send()
+        z_sent((2, 3))
 
     dma = pltpu.SemaphoreType.DMA
     scratch = [
@@ -392,8 +407,8 @@
         pltpu.VMEM((npix, ngal), bf16),
         pltpu.VMEM((shifts, npix), bf16),
         pltpu.VMEM((2, NX, far, TP, quarter), bf16),
-        pltpu.VMEM((2, NX, far - 1, TP, quarter), bf16),
-        pltpu.VMEM((2, NX, TP, quarter), bf16),
+        pltpu.VMEM((2, NX, 2, TP, quarter), bf16),
+        pltpu.VMEM((3, NX, TP, quarter), bf16),
         pltpu.VMEM((zpix, quarter), bf16),
         pltpu.VMEM((NX, TP, quarter), bf16),
         pltpu.VMEM((NX, 1, 2 * SW), f32),
@@ -403,7 +418,7 @@
     ]
     for shape in ((NX,), (3, NX), (chan_size,), (chan_size,), (NX,)):
         scratch += [dma(shape), dma(shape)]
-    scratch += [dma((2, NX, far)), dma((2, NX, far - 1)), dma((2, NX))]
+    scratch += [dma((2, NX, far)), dma((2, NX, 2)), dma((3, NX))]
     for shape in ((NX,), (NX,), (chan_size,), (nz,)):
         scratch += [dma(shape), dma(shape)]
     return kernel, scratch

time: 44.5 us -> 45.3 us (1.018)
  Pallas kernels: 41.8 us -> 42.6 us
    pallas_call x1, Pallas kernels: 41.8 us -> 42.6 us  [per_device(): pl.pallas_call(kernel, out_shape=(jax.ShapeDtypeStruct((TP, width), bf16)...]
where the time goes in v5:
time: 45.3 us; the launch traced here: 45.2 us
  Pallas kernels  42.6 us (94%)
  local copies, waits for them, and re-layouts  1.86 us (4%)
  between operations  0.69 us (2%)
    pallas_call x1, Pallas kernels, per_device(): pl.pallas_call(kernel, out_shape=(jax.ShapeDtypeStruct((TP, width), bf16)...  42.6 us
    unnamed x14, local copies, waits for them, and re-layouts  1.86 us

profile of v5, /device:TPU:1, one launch (start us, length us, event | category | flops | bytes accessed | tf_op | source)
XLA Modules:
  0.0 45.2 jit_solution(6698541360082597316)
XLA Ops:
  0.6 0.0 copy-start.3
  0.6 0.0 copy-start.5
  0.7 0.0 copy-start
  0.7 0.0 copy-start.1
  0.7 0.0 copy-start.2
  0.7 0.0 copy-start.4
  0.7 0.6 %copy-done.3 = s32[256]{0:T(256)S(1)} copy-done((s32[256]{0:T(256)S(1)}, s32[256]{0:T(256)}, u32[]{:S(2)}) %copy-start.3) | copy-done | bytes 1048
  1.3 0.0 copy-done.5
  1.3 0.0 copy-done
  1.4 0.0 copy-done.1
  1.4 0.0 copy-done.2
  1.4 0.0 copy-done.4
  1.4 42.6 %shard_map.95 = (bf16[64,1024]{1,0:T(8,128)(2,1)S(1)}, f32[1,128]{1,0:T(1,128)S(1)}) custom-call(bf16[512,1024]{1,0:T(8,128)(2,1)} %spec.1, f32[16,8192]{1,0:T(8,128)} %constant.2.clone.basis_in, f32[1,1024]{1,0:T(1,128)S(1)} %bitcast.7, s32[1,32]{1,0:T(1,128)S(1)} %bitcast.11, s32[1,512]{1,0:T(1,128)S(1)} %bitcast.8, bf16[1,16]{1,0:T(2,128)(2,1)S(1)} %bitcast.12, ...), custom_call_target="tpu_custom_call" | custom-call | tf_op jit(solution)/shard_map/pallas_call | solution.py:437
  44.0 0.7 %copy.12 = bf16[64,1024]{1,0:T(8,128)(2,1)} copy(bf16[64,1024]{1,0:T(8,128)(2,1)S(1)} %get-tuple-element.8) | data formatting | bytes 262144
  44.7 0.5 %copy.13 = f32[128]{0:T(128)} copy(f32[128]{0:T(128)S(1)} %bitcast.13) | data formatting | bytes 1024
Async XLA Ops:
  0.6 0.7 %copy-start.3 = (s32[256]{0:T(256)S(1)}, s32[256]{0:T(256)}, u32[]{:S(2)}) copy-start(s32[256]{0:T(256)} %param.14) | copy-start | bytes 3076
  0.6 0.7 %copy-start.5 = (bf16[16]{0:T(256)(128)(2,1)S(1)}, bf16[16]{0:T(256)(128)(2,1)}, u32[]{:S(2)}) copy-start(bf16[16]{0:T(256)(128)(2,1)} %param.12) | copy-start | bytes 100
  0.7 0.7 %copy-start = (f32[1024]{0:T(1024)S(1)}, f32[1024]{0:T(1024)}, u32[]{:S(2)}) copy-start(f32[1024]{0:T(1024)} %param.9) | copy-start | bytes 12292
  0.7 0.7 %copy-start.1 = (s32[512]{0:T(512)S(1)}, s32[512]{0:T(512)}, u32[]{:S(2)}) copy-start(s32[512]{0:T(512)} %param.11) | copy-start | bytes 6148
  0.7 0.7 %copy-start.2 = (s32[256]{0:T(256)S(1)}, s32[256]{0:T(256)}, u32[]{:S(2)}) copy-start(s32[256]{0:T(256)} %param.13) | copy-start | bytes 3076
  0.7 0.7 %copy-start.4 = (s32[32,1]{0,1:T(1,128)S(1)}, s32[32,1]{0,1:T(1,128)}, u32[]{:S(2)}) copy-start(s32[32,1]{0,1:T(1,128)} %param.10) | copy-start | bytes 388

commit v6 on v2

--- a/solution.py
+++ b/solution.py
@@ -50,7 +50,7 @@
     def kernel(
         spec, basis_in, weight, routes, offsets, taps, gal_pix, gal_chan,
         sky, stacked,
-        own, basis, pix, raw, gram, proj, ext, coef, band, ripple, clean, part, pixel_hot, counts,
+        own, basis, pix, raw, gram, proj, ext, coef, band, ripple, clean, part, pixel_hot, counts, seen,
         zsend, zrecv, edge, final, mine, st1, st2, st3,
         load_sem, pix_s, pix_r, raw_s, raw_r, gram_s, gram_r, proj_s, proj_r, coef_s, coef_r,
         z_s, z_r, edge_r, mine_s, mine_r, st1_s, st1_r, st2_s, st2_r, st3_s, st3_r,
@@ -111,6 +111,10 @@
         )[0:1].astype(jnp.int32)
         pix[0] = tile * TP + offsets[...] - MARGIN
 
+        loads[1].wait()
+        weighted = basis[...] * weight[...]
+        w_stack = jnp.concatenate(split3(weighted), axis=0)
+
         pl.semaphore_wait(barrier, len(peers))
         for r in range(1, NX):
             start(remote(pix.at[0], pix.at[NX - r], pix_s.at[r], pix_r.at[NX - r], x_peer(r)))
@@ -121,17 +125,14 @@
             column = pl.multiple_of(lax.rem(x + r, NX) * quarter, quarter)
             low, high = ((0, late), (late, rows), (0, rows))[piece]
             return remote(
-                spec.at[low:high, pl.ds(column, quarter)], raw.at[NX - r, low:high],
+                own.at[low:high, pl.ds(column, quarter)], raw.at[NX - r, low:high],
                 raw_s.at[piece, r], raw_r.at[piece, NX - r], x_peer(r),
             )
 
+        loads[0].wait()
         for r, piece in ((2, 2), (1, 0), (3, 0)):
             start(raw_copy(r, piece))
 
-        loads[1].wait()
-        weighted = basis[...] * weight[...]
-        w_stack = jnp.concatenate(split3(weighted), axis=0)
-        loads[0].wait()
         products = lax.dot_general(
             w_stack, own[...], (((1,), (1,)), ((), ())), preferred_element_type=f32
         )
@@ -237,6 +238,14 @@
         for r in range(1, NX):
             remote(pix.at[0], pix.at[r], pix_s.at[r], pix_r.at[r], x_peer(r)).wait_recv()
             build_band(r)
+        def weigh(slot, carry):
+            column = pl.multiple_of(slot * rows, rows)
+            seen[:, pl.ds(column, rows)] = jnp.dot(
+                counts[...], band[:, pl.ds(column, rows)], preferred_element_type=f32
+            ).astype(bf16)
+            return carry
+
+        lax.fori_loop(0, NX, weigh, 0)
         for r in (1, 3, 2):
             remote(coef.at[0], coef.at[r], coef_s.at[r], coef_r.at[r], x_peer(r)).wait_recv()
             fit_slot(r)
@@ -279,33 +288,17 @@
                     zsend[way, tile, k] = value.astype(bf16)
                     z_copy(way, tile, k).start()
 
-        def z_sent(last):
-            for way in range(2):
-                for tile in range(NX):
-                    count = hops(way, tile)
-                    for k in (count - 1,) if last else range(count - 1):
-                        z_copy(way, tile, k).wait_send()
-
-        def grid_step(n, carry):
-            away = lax.div(n + 1, 2)
-            row = chunk_row(far + away - 2 * lax.rem(n, 2) * away)
-            part[pl.ds(row, zpix), :] = jnp.dot(
-                band[pl.ds(row, zpix), :], clean[...], preferred_element_type=f32
-            )
-
-            @pl.when(n == 0)
-            def _():
-                z_step(0, True)
-
-            @pl.when(n == 2)
-            def _():
-                z_step(0, False)
-
-            return carry
-
         def share(buffer, me, send_sem, recv_sem, peer_of, count):
             for r in range(1, count):
-                start(remote(buffer.at[me], buffer.at[me], send_sem.at[r], recv_sem.at[me], peer_of(r)))
+                remote(
+                    buffer.at[me], buffer.at[me], send_sem.at[r], recv_sem.at[me], peer_of(r)
+                ).start()
+
+        def shared(buffer, me, send_sem, recv_sem, peer_of, count):
+            for r in range(1, count):
+                remote(
+                    buffer.at[me], buffer.at[me], send_sem.at[r], recv_sem.at[me], peer_of(r)
+                ).wait_send()
 
         def gather(buffer, me, send_sem, recv_sem, peer_of, count):
             for r in range(1, count):
@@ -318,25 +311,51 @@
                 value = value + buffer[i]
             return value
 
+        def stack_part():
+            wide = jnp.concatenate(
+                [
+                    jnp.dot(seen[...], clean[...], preferred_element_type=f32),
+                    jnp.zeros((shifts, 512 - quarter), f32),
+                ],
+                axis=1,
+            )
+            folded = jnp.zeros((8, 512), f32)
+            for i in range(shifts // 8):
+                folded = folded + pltpu.roll(
+                    wide[8 * i:8 * i + 8], (513 - quarter + 8 * i) % 512, 1
+                )
+            window = jnp.zeros((1, 512), f32)
+            for i in range(8):
+                window = window + (pltpu.roll(folded[i:i + 1], i, 1) if i else folded[i:i + 1])
+            st1[x] = window[:, :2 * SW]
+            share(st1, x, st1_s, st1_r, x_peer, NX)
+
+        def z_sent(last):
+            for way in range(2):
+                for tile in range(NX):
+                    count = hops(way, tile)
+                    for k in (count - 1,) if last else range(count - 1):
+                        z_copy(way, tile, k).wait_send()
+
+        def grid_step(n, carry):
+            away = lax.div(n + 1, 2)
+            row = chunk_row(far + away - 2 * lax.rem(n, 2) * away)
+            part[pl.ds(row, zpix), :] = jnp.dot(
+                band[pl.ds(row, zpix), :], clean[...], preferred_element_type=f32
+            )
+
+            @pl.when(n == 0)
+            def _():
+                z_step(0, True)
+                stack_part()
+
+            @pl.when(n == 2)
+            def _():
+                z_step(0, False)
+
+            return carry
+
         lax.fori_loop(0, nz, grid_step, 0)
-
-        wide = jnp.concatenate(
-            [
-                jnp.dot(counts[...], part[...].astype(bf16), preferred_element_type=f32),
-                jnp.zeros((shifts, 512 - quarter), f32),
-            ],
-            axis=1,
-        )
-        folded = jnp.zeros((8, 512), f32)
-        for i in range(shifts // 8):
-            folded = folded + pltpu.roll(
-                wide[8 * i:8 * i + 8], (513 - quarter + 8 * i) % 512, 1
-            )
-        window = jnp.zeros((1, 512), f32)
-        for i in range(8):
-            window = window + (pltpu.roll(folded[i:i + 1], i, 1) if i else folded[i:i + 1])
-        st1[x] = window[:, :2 * SW]
-        share(st1, x, st1_s, st1_r, x_peer, NX)
 
         z_step(1, True)
         z_step(1, False)
@@ -360,6 +379,8 @@
             ).wait_recv()
         for copy in sends:
             copy.wait_send()
+        shared(st1, x, st1_s, st1_r, x_peer, NX)
+        shared(st2, j, st2_s, st2_r, c_peer, chan_size)
         z_sent(False)
 
         for way in range(2):
@@ -379,6 +400,7 @@
             sky[:, pl.ds(column, quarter)] = value.astype(bf16)
         stacked[...] = gather(st3, z, st3_s, st3_r, z_peer, nz) / ngal
         z_sent(True)
+        shared(st3, z, st3_s, st3_r, z_peer, nz)
 
     dma = pltpu.SemaphoreType.DMA
     scratch = [
@@ -396,6 +418,7 @@
         pltpu.VMEM((npix, quarter), f32),
         pltpu.VMEM((npix, ngal), bf16),
         pltpu.VMEM((shifts, npix), bf16),
+        pltpu.VMEM((shifts, NX * rows), bf16),
         pltpu.VMEM((2, NX, far, TP, quarter), bf16),
         pltpu.VMEM((2, NX, far - 1, TP, quarter), bf16),
         pltpu.VMEM((2, NX, TP, quarter), bf16),

time: 44.6 us -> 45.6 us (1.022)
  Pallas kernels: 41.9 us -> 42.5 us
    pallas_call x1, Pallas kernels: 41.9 us -> 42.5 us  [per_device(): pl.pallas_call(kernel, out_shape=(jax.ShapeDtypeStruct((TP, width), bf16)...]
where the time goes in v6:
time: 45.6 us; the launch traced here: 45 us
  Pallas kernels  42.5 us (93%)
  local copies, waits for them, and re-layouts  1.86 us (4%)
  between operations  0.69 us (2%)
    pallas_call x1, Pallas kernels, per_device(): pl.pallas_call(kernel, out_shape=(jax.ShapeDtypeStruct((TP, width), bf16)...  42.5 us
    unnamed x14, local copies, waits for them, and re-layouts  1.86 us

profile of v6, /device:TPU:1, one launch (start us, length us, event | category | flops | bytes accessed | tf_op | source)
XLA Modules:
  0.0 45.0 jit_solution(2693309926577218069)
XLA Ops:
  0.6 0.0 copy-start.3
  0.6 0.0 copy-start.5
  0.7 0.0 copy-start
  0.7 0.0 copy-start.1
  0.7 0.0 copy-start.2
  0.7 0.0 copy-start.4
  0.7 0.6 %copy-done.3 = s32[256]{0:T(256)S(1)} copy-done((s32[256]{0:T(256)S(1)}, s32[256]{0:T(256)}, u32[]{:S(2)}) %copy-start.3) | copy-done | bytes 1048
  1.3 0.0 copy-done.5
  1.3 0.0 copy-done
  1.4 0.0 copy-done.1
  1.4 0.0 copy-done.2
  1.4 0.0 copy-done.4
  1.4 42.5 %shard_map.95 = (bf16[64,1024]{1,0:T(8,128)(2,1)S(1)}, f32[1,128]{1,0:T(1,128)S(1)}) custom-call(bf16[512,1024]{1,0:T(8,128)(2,1)} %spec.1, f32[16,8192]{1,0:T(8,128)} %constant.2.clone.basis_in, f32[1,1024]{1,0:T(1,128)S(1)} %bitcast.7, s32[1,32]{1,0:T(1,128)S(1)} %bitcast.11, s32[1,512]{1,0:T(1,128)S(1)} %bitcast.8, bf16[1,16]{1,0:T(2,128)(2,1)S(1)} %bitcast.12, ...), custom_call_target="tpu_custom_call" | custom-call | tf_op jit(solution)/shard_map/pallas_call | solution.py:450
  43.9 0.7 %copy.12 = bf16[64,1024]{1,0:T(8,128)(2,1)} copy(bf16[64,1024]{1,0:T(8,128)(2,1)S(1)} %get-tuple-element.8) | data formatting | bytes 262144
  44.5 0.5 %copy.13 = f32[128]{0:T(128)} copy(f32[128]{0:T(128)S(1)} %bitcast.13) | data formatting | bytes 1024
Async XLA Ops:
  0.6 0.7 %copy-start.3 = (s32[256]{0:T(256)S(1)}, s32[256]{0:T(256)}, u32[]{:S(2)}) copy-start(s32[256]{0:T(256)} %param.14) | copy-start | bytes 3076
  0.6 0.7 %copy-start.5 = (bf16[16]{0:T(256)(128)(2,1)S(1)}, bf16[16]{0:T(256)(128)(2,1)}, u32[]{:S(2)}) copy-start(bf16[16]{0:T(256)(128)(2,1)} %param.12) | copy-start | bytes 100
  0.7 0.7 %copy-start = (f32[1024]{0:T(1024)S(1)}, f32[1024]{0:T(1024)}, u32[]{:S(2)}) copy-start(f32[1024]{0:T(1024)} %param.9) | copy-start | bytes 12292
  0.7 0.7 %copy-start.1 = (s32[512]{0:T(512)S(1)}, s32[512]{0:T(512)}, u32[]{:S(2)}) copy-start(s32[512]{0:T(512)} %param.11) | copy-start | bytes 6148
  0.7 0.7 %copy-start.2 = (s32[256]{0:T(256)S(1)}, s32[256]{0:T(256)}, u32[]{:S(2)}) copy-start(s32[256]{0:T(256)} %param.13) | copy-start | bytes 3076
  0.7 0.7 %copy-start.4 = (s32[32,1]{0,1:T(1,128)S(1)}, s32[32,1]{0,1:T(1,128)}, u32[]{:S(2)}) copy-start(s32[32,1]{0,1:T(1,128)} %param.10) | copy-start | bytes 388

commit v7 on v3

--- a/solution.py
+++ b/solution.py
@@ -50,7 +50,7 @@
     def kernel(
         spec, basis_in, weight, routes, offsets, taps, gal_pix, gal_chan,
         sky, stacked,
-        own, basis, pix, raw, gram, proj, ext, coef, band, clean, part, pixel_hot, counts,
+        own, basis, pix, raw, gram, proj, ext, coef, band, ripple, clean, part, pixel_hot, counts,
         zsend, zrecv, edge, final, mine, st1, st2, st3,
         load_sem, pix_s, pix_r, raw_s, raw_r, gram_s, gram_r, proj_s, proj_r, coef_s, coef_r,
         z_s, z_r, edge_r, mine_s, mine_r, st1_s, st1_r, st2_s, st2_r, st3_s, st3_r,
@@ -180,6 +180,21 @@
 
         build_band(0)
 
+        begin = gal_chan[...] - SW - (j * width + here)
+        shift_hot = (iota((shifts, ngal), 0) == quarter - 1 - begin).astype(f32).astype(bf16)
+        gal_row = jnp.broadcast_to(gal_pix[...], (TAPS, ngal))
+        fill(
+            pixel_hot, 0, gal_row >> 4,
+            jnp.where((gal_row & (TAPS - 1)) == iota((TAPS, ngal), 0), 1.0, 0.0).astype(f32),
+        )
+        counts[...] = lax.dot_general(
+            shift_hot, pixel_hot[...], (((1,), (1,)), ((), ())), preferred_element_type=f32
+        ).astype(bf16)
+
+        for r in range(1, NX):
+            remote(pix.at[0], pix.at[r], pix_s.at[r], pix_r.at[r], x_peer(r)).wait_recv()
+            build_band(r)
+
         for r in range(1, chan_size):
             remote(gram.at[0], gram.at[r], gram_s.at[r], gram_r.at[r], c_peer(r)).wait_recv()
         total = gram[0]
@@ -201,6 +216,7 @@
         coef[0] = jnp.dot(both, ext[...], precision=highest, preferred_element_type=f32)
         for r in range(1, NX):
             start(remote(coef.at[0], coef.at[NX - r], coef_s.at[r], coef_r.at[NX - r], x_peer(r)))
+
         for r in (1, 3):
             start(raw_copy(r, 1))
 
@@ -210,37 +226,30 @@
             axis=0,
         )
 
-        def clean_slot(slot, values):
+        def fit_slot(slot):
             c_high, c_mid, c_low = split3(coef[slot])
             c_stack = jnp.concatenate(
                 [c_high, c_high, c_mid, c_mid, c_high, c_low, jnp.zeros((2 * MODES, rows), bf16)],
                 axis=0,
             )
-            ripple = lax.dot_general(
+            ripple[slot * rows:(slot + 1) * rows, :] = lax.dot_general(
                 c_stack, b_stack, (((0,), (0,)), ((), ())), preferred_element_type=f32
             )
-            clean[slot * rows:(slot + 1) * rows, :] = (values.astype(f32) - ripple).astype(bf16)
-
+
+        def clean_slot(slot, values):
+            clean[slot * rows:(slot + 1) * rows, :] = (
+                values.astype(f32) - ripple[slot * rows:(slot + 1) * rows, :]
+            ).astype(bf16)
+
+        fit_slot(0)
         clean_slot(0, own[0:rows, pl.ds(here, quarter)])
 
-        begin = gal_chan[...] - SW - (j * width + here)
-        shift_hot = (iota((shifts, ngal), 0) == quarter - 1 - begin).astype(f32).astype(bf16)
-        gal_row = jnp.broadcast_to(gal_pix[...], (TAPS, ngal))
-        fill(
-            pixel_hot, 0, gal_row >> 4,
-            jnp.where((gal_row & (TAPS - 1)) == iota((TAPS, ngal), 0), 1.0, 0.0).astype(f32),
-        )
-        counts[...] = lax.dot_general(
-            shift_hot, pixel_hot[...], (((1,), (1,)), ((), ())), preferred_element_type=f32
-        ).astype(bf16)
-
-        for r in range(1, NX):
-            remote(pix.at[0], pix.at[r], pix_s.at[r], pix_r.at[r], x_peer(r)).wait_recv()
-            build_band(r)
-        for r, pieces in ((1, (0, 1)), (3, (0, 1)), (2, (2,))):
+        for r in (1, 3, 2):
+            remote(coef.at[0], coef.at[r], coef_s.at[r], coef_r.at[r], x_peer(r)).wait_recv()
+            fit_slot(r)
+        for r, pieces in ((2, (2,)), (1, (0, 1)), (3, (0, 1))):
             for piece in pieces:
                 raw_copy(NX - r, piece).wait_recv()
-            remote(coef.at[0], coef.at[r], coef_s.at[r], coef_r.at[r], x_peer(r)).wait_recv()
             clean_slot(r, raw[r])
 
         def chunk_row(step):
@@ -389,6 +398,7 @@
         pltpu.VMEM((128, rows), f32),
         pltpu.VMEM((NX, MODES, rows), f32),
         pltpu.VMEM((npix, NX * rows), bf16),
+        pltpu.VMEM((NX * rows, quarter), f32),
         pltpu.VMEM((NX * rows, quarter), bf16),
         pltpu.VMEM((npix, quarter), f32),
         pltpu.VMEM((npix, ngal), bf16),

time: 45.2 us -> 44.8 us (level)
  no operation moved by 1% of the time
where the time goes in v7:
time: 44.8 us; the launch traced here: 44.7 us
  Pallas kernels  42.2 us (94%)
  local copies, waits for them, and re-layouts  1.86 us (4%)
  between operations  0.69 us (2%)
    pallas_call x1, Pallas kernels, per_device(): pl.pallas_call(kernel, out_shape=(jax.ShapeDtypeStruct((TP, width), bf16)...  42.2 us
    unnamed x14, local copies, waits for them, and re-layouts  1.86 us

profile of v7, /device:TPU:1, one launch (start us, length us, event | category | flops | bytes accessed | tf_op | source)
XLA Modules:
  0.0 44.7 jit_solution(15206456889630387078)
XLA Ops:
  0.6 0.0 copy-start.3
  0.6 0.0 copy-start.5
  0.7 0.0 copy-start
  0.7 0.0 copy-start.1
  0.7 0.0 copy-start.2
  0.7 0.0 copy-start.4
  0.7 0.6 %copy-done.3 = s32[256]{0:T(256)S(1)} copy-done((s32[256]{0:T(256)S(1)}, s32[256]{0:T(256)}, u32[]{:S(2)}) %copy-start.3) | copy-done | bytes 1048
  1.3 0.0 copy-done.5
  1.3 0.0 copy-done
  1.4 0.0 copy-done.1
  1.4 0.0 copy-done.2
  1.4 0.0 copy-done.4
  1.4 42.2 %shard_map.95 = (bf16[64,1024]{1,0:T(8,128)(2,1)S(1)}, f32[1,128]{1,0:T(1,128)S(1)}) custom-call(bf16[512,1024]{1,0:T(8,128)(2,1)} %spec.1, f32[16,8192]{1,0:T(8,128)} %constant.2.clone.basis_in, f32[1,1024]{1,0:T(1,128)S(1)} %bitcast.7, s32[1,32]{1,0:T(1,128)S(1)} %bitcast.11, s32[1,512]{1,0:T(1,128)S(1)} %bitcast.8, bf16[1,16]{1,0:T(2,128)(2,1)S(1)} %bitcast.12, ...), custom_call_target="tpu_custom_call" | custom-call | tf_op jit(solution)/shard_map/pallas_call | solution.py:434
  43.6 0.7 %copy.12 = bf16[64,1024]{1,0:T(8,128)(2,1)} copy(bf16[64,1024]{1,0:T(8,128)(2,1)S(1)} %get-tuple-element.8) | data formatting | bytes 262144
  44.2 0.5 %copy.13 = f32[128]{0:T(128)} copy(f32[128]{0:T(128)S(1)} %bitcast.13) | data formatting | bytes 1024
Async XLA Ops:
  0.6 0.7 %copy-start.3 = (s32[256]{0:T(256)S(1)}, s32[256]{0:T(256)}, u32[]{:S(2)}) copy-start(s32[256]{0:T(256)} %param.14) | copy-start | bytes 3076
  0.6 0.7 %copy-start.5 = (bf16[16]{0:T(256)(128)(2,1)S(1)}, bf16[16]{0:T(256)(128)(2,1)}, u32[]{:S(2)}) copy-start(bf16[16]{0:T(256)(128)(2,1)} %param.12) | copy-start | bytes 100
  0.7 0.7 %copy-start = (f32[1024]{0:T(1024)S(1)}, f32[1024]{0:T(1024)}, u32[]{:S(2)}) copy-start(f32[1024]{0:T(1024)} %param.9) | copy-start | bytes 12292
  0.7 0.7 %copy-start.1 = (s32[512]{0:T(512)S(1)}, s32[512]{0:T(512)}, u32[]{:S(2)}) copy-start(s32[512]{0:T(512)} %param.11) | copy-start | bytes 6148
  0.7 0.7 %copy-start.2 = (s32[256]{0:T(256)S(1)}, s32[256]{0:T(256)}, u32[]{:S(2)}) copy-start(s32[256]{0:T(256)} %param.13) | copy-start | bytes 3076
  0.7 0.7 %copy-start.4 = (s32[32,1]{0,1:T(1,128)S(1)}, s32[32,1]{0,1:T(1,128)}, u32[]{:S(2)}) copy-start(s32[32,1]{0,1:T(1,128)} %param.10) | copy-start | bytes 388

commit v8 on v7

--- a/solution.py
+++ b/solution.py
@@ -50,7 +50,7 @@
     def kernel(
         spec, basis_in, weight, routes, offsets, taps, gal_pix, gal_chan,
         sky, stacked,
-        own, basis, pix, raw, gram, proj, ext, coef, band, ripple, clean, part, pixel_hot, counts,
+        own, basis, pix, raw, gram, proj, coef, band, ripple, clean, part, pixel_hot, counts,
         zsend, zrecv, edge, final, mine, st1, st2, st3,
         load_sem, pix_s, pix_r, raw_s, raw_r, gram_s, gram_r, proj_s, proj_r, coef_s, coef_r,
         z_s, z_r, edge_r, mine_s, mine_r, st1_s, st1_r, st2_s, st2_r, st3_s, st3_r,
@@ -164,7 +164,7 @@
                 ).astype(bf16)
                 return carry
 
-            lax.fori_loop(0, npix // TAPS, step, 0, unroll=4)
+            lax.fori_loop(0, npix // TAPS, step, 0, unroll=8)
 
         def build_band(slot):
             first = pix[slot]
@@ -182,13 +182,13 @@
 
         begin = gal_chan[...] - SW - (j * width + here)
         shift_hot = (iota((shifts, ngal), 0) == quarter - 1 - begin).astype(f32).astype(bf16)
-        gal_row = jnp.broadcast_to(gal_pix[...], (TAPS, ngal))
-        fill(
-            pixel_hot, 0, gal_row >> 4,
-            jnp.where((gal_row & (TAPS - 1)) == iota((TAPS, ngal), 0), 1.0, 0.0).astype(f32),
-        )
-        counts[...] = lax.dot_general(
-            shift_hot, pixel_hot[...], (((1,), (1,)), ((), ())), preferred_element_type=f32
+        gal_column = jnp.broadcast_to(gal_pix[...].astype(f32), (128, ngal)).T.astype(jnp.int32)
+        for i in range(npix // 128):
+            pixel_hot[:, 128 * i:128 * (i + 1)] = jnp.where(
+                gal_column - 128 * i == iota((ngal, 128), 1), 1.0, 0.0
+            ).astype(bf16)
+        counts[...] = jnp.dot(
+            shift_hot, pixel_hot[...], preferred_element_type=f32
         ).astype(bf16)
 
         for r in range(1, NX):
@@ -206,14 +206,15 @@
             pivot = both[i:i + 1, :] / both[i:i + 1, i:i + 1]
             both = jnp.where(row_id == i, pivot, both - both[:, i:i + 1] * pivot)
 
-        ext[...] = jnp.zeros(ext.shape, f32)
         for r in range(1, chan_size):
             remote(proj.at[0], proj.at[r], proj_s.at[r], proj_r.at[r], c_peer(r)).wait_recv()
         full = proj[0]
         for r in range(1, chan_size):
             full = full + proj[r]
-        ext[MODES:2 * MODES, :] = full
-        coef[0] = jnp.dot(both, ext[...], precision=highest, preferred_element_type=f32)
+        solved = both[:, MODES:MODES + 1] * full[0:1, :]
+        for i in range(1, MODES):
+            solved = solved + both[:, MODES + i:MODES + i + 1] * full[i:i + 1, :]
+        coef[0] = solved
         for r in range(1, NX):
             start(remote(coef.at[0], coef.at[NX - r], coef_s.at[r], coef_r.at[NX - r], x_peer(r)))
 
@@ -395,13 +396,12 @@
         pltpu.VMEM((NX, rows, quarter), bf16),
         pltpu.VMEM((chan_size, MODES, 128), f32),
         pltpu.VMEM((chan_size, MODES, rows), f32),
-        pltpu.VMEM((128, rows), f32),
         pltpu.VMEM((NX, MODES, rows), f32),
         pltpu.VMEM((npix, NX * rows), bf16),
         pltpu.VMEM((NX * rows, quarter), f32),
         pltpu.VMEM((NX * rows, quarter), bf16),
         pltpu.VMEM((npix, quarter), f32),
-        pltpu.VMEM((npix, ngal), bf16),
+        pltpu.VMEM((ngal, npix), bf16),
         pltpu.VMEM((shifts, npix), bf16),
         pltpu.VMEM((2, NX, far, TP, quarter), bf16),
         pltpu.VMEM((2, NX, far - 1, TP, quarter), bf16),

time: 44.8 us -> 44.6 us (level)
  no operation moved by 1% of the time
where the time goes in v8:
time: 44.6 us; the launch traced here: 44.5 us
  Pallas kernels  41.9 us (94%)
  local copies, waits for them, and re-layouts  1.86 us (4%)
  between operations  0.69 us (2%)
    pallas_call x1, Pallas kernels, per_device(): pl.pallas_call(kernel, out_shape=(jax.ShapeDtypeStruct((TP, width), bf16)...  41.9 us
    unnamed x14, local copies, waits for them, and re-layouts  1.86 us

profile of v8, /device:TPU:1, one launch (start us, length us, event | category | flops | bytes accessed | tf_op | source)
XLA Modules:
  0.0 44.5 jit_solution(3304610528513480138)
XLA Ops:
  0.6 0.0 copy-start.3
  0.6 0.0 copy-start.5
  0.7 0.0 copy-start
  0.7 0.0 copy-start.1
  0.7 0.0 copy-start.2
  0.7 0.0 copy-start.4
  0.7 0.6 %copy-done.3 = s32[256]{0:T(256)S(1)} copy-done((s32[256]{0:T(256)S(1)}, s32[256]{0:T(256)}, u32[]{:S(2)}) %copy-start.3) | copy-done | bytes 1048
  1.3 0.0 copy-done.5
  1.3 0.0 copy-done
  1.4 0.0 copy-done.1
  1.4 0.0 copy-done.2
  1.4 0.0 copy-done.4
  1.4 41.9 %shard_map.95 = (bf16[64,1024]{1,0:T(8,128)(2,1)S(1)}, f32[1,128]{1,0:T(1,128)S(1)}) custom-call(bf16[512,1024]{1,0:T(8,128)(2,1)} %spec.1, f32[16,8192]{1,0:T(8,128)} %constant.2.clone.basis_in, f32[1,1024]{1,0:T(1,128)S(1)} %bitcast.7, s32[1,32]{1,0:T(1,128)S(1)} %bitcast.11, s32[1,512]{1,0:T(1,128)S(1)} %bitcast.8, bf16[1,16]{1,0:T(2,128)(2,1)S(1)} %bitcast.12, ...), custom_call_target="tpu_custom_call" | custom-call | tf_op jit(solution)/shard_map/pallas_call | solution.py:434
  43.3 0.7 %copy.12 = bf16[64,1024]{1,0:T(8,128)(2,1)} copy(bf16[64,1024]{1,0:T(8,128)(2,1)S(1)} %get-tuple-element.8) | data formatting | bytes 262144
  44.0 0.5 %copy.13 = f32[128]{0:T(128)} copy(f32[128]{0:T(128)S(1)} %bitcast.13) | data formatting | bytes 1024
Async XLA Ops:
  0.6 0.7 %copy-start.3 = (s32[256]{0:T(256)S(1)}, s32[256]{0:T(256)}, u32[]{:S(2)}) copy-start(s32[256]{0:T(256)} %param.14) | copy-start | bytes 3076
  0.6 0.7 %copy-start.5 = (bf16[16]{0:T(256)(128)(2,1)S(1)}, bf16[16]{0:T(256)(128)(2,1)}, u32[]{:S(2)}) copy-start(bf16[16]{0:T(256)(128)(2,1)} %param.12) | copy-start | bytes 100
  0.7 0.7 %copy-start = (f32[1024]{0:T(1024)S(1)}, f32[1024]{0:T(1024)}, u32[]{:S(2)}) copy-start(f32[1024]{0:T(1024)} %param.9) | copy-start | bytes 12292
  0.7 0.7 %copy-start.1 = (s32[512]{0:T(512)S(1)}, s32[512]{0:T(512)}, u32[]{:S(2)}) copy-start(s32[512]{0:T(512)} %param.11) | copy-start | bytes 6148
  0.7 0.7 %copy-start.2 = (s32[256]{0:T(256)S(1)}, s32[256]{0:T(256)}, u32[]{:S(2)}) copy-start(s32[256]{0:T(256)} %param.13) | copy-start | bytes 3076
  0.7 0.7 %copy-start.4 = (s32[32,1]{0,1:T(1,128)S(1)}, s32[32,1]{0,1:T(1,128)}, u32[]{:S(2)}) copy-start(s32[32,1]{0,1:T(1,128)} %param.10) | copy-start | bytes 388

commit v9 on v8

--- a/solution.py
+++ b/solution.py
@@ -70,8 +70,8 @@
         def z_peer(r):
             return (lax.rem(z + r, nz) * NX + x, j)
 
-        def beside(way, place):
-            return (lax.rem(place[0] + (NX, (nz - 1) * NX)[way], tm_size), place[1])
+        def beside(way, place, away):
+            return (lax.rem(place[0] + (away, nz - away)[way] * NX, tm_size), place[1])
 
         def remote(src, dst, send_sem, recv_sem, peer):
             return pltpu.make_async_remote_copy(
@@ -89,7 +89,11 @@
             [x_peer(r) for r in range(1, NX)]
             + [c_peer(r) for r in range(1, chan_size)]
             + [z_peer(r) for r in range(1, nz)]
-            + [beside(way, x_peer(r)) for way in range(2) for r in range(1, NX)]
+            + [beside(way, x_peer(r), 1) for way in range(2) for r in range(1, NX)]
+            + [
+                (lax.rem(z + nz - 2 + 4 * lax.div(x, 2), nz) * NX + lax.rem(x + r, NX), j)
+                for r in range(1, NX)
+            ]
         )
         barrier = pltpu.get_barrier_semaphore()
         for peer in peers:
@@ -262,16 +266,21 @@
 
         sign = (1, -1)
 
-        def hops(way, tile):
-            return far if tile // 2 == way else far - 1
+        def distance(way, tile, k):
+            long = tile // 2 == way
+            return (far, far - 1, far - 2, 1)[k] if long else (far - 1, far - 2, 1)[k]
+
+        def steps(way, tile):
+            return 4 if tile // 2 == way else 3
 
         def z_copy(way, tile, k):
-            if k < hops(way, tile) - 1:
+            if k < 2:
                 target, recv_sem = zrecv.at[way, tile, k], z_r.at[way, tile, k]
                 peer = z_peer((1, nz - 1)[way])
             else:
-                target, recv_sem = edge.at[way, x], edge_r.at[way, x]
-                peer = beside(way, (z * NX + tile, j))
+                slot = way if k == 2 else 2
+                target, recv_sem = edge.at[slot, x], edge_r.at[slot, x]
+                peer = beside(way, (z * NX + tile, j), distance(way, tile, k))
             return remote(
                 zsend.at[way, tile, k], target, z_s.at[way, tile, k], recv_sem, peer
             )
@@ -280,19 +289,19 @@
             for lane in range(2):
                 for way in range(2):
                     tile = 2 * (way if long else 1 - way) + lane
-                    value = part_tile(sign[way] * (hops(way, tile) - k), tile)
-                    if k:
+                    value = part_tile(sign[way] * distance(way, tile, k), tile)
+                    if k in (1, 2):
                         z_copy(way, tile, k - 1).wait_recv()
                         value = value + zrecv[way, tile, k - 1].astype(f32)
                     zsend[way, tile, k] = value.astype(bf16)
                     z_copy(way, tile, k).start()
 
-        def z_sent(last):
+        def z_sent(ks):
             for way in range(2):
                 for tile in range(NX):
-                    count = hops(way, tile)
-                    for k in (count - 1,) if last else range(count - 1):
-                        z_copy(way, tile, k).wait_send()
+                    for k in ks:
+                        if k < steps(way, tile):
+                            z_copy(way, tile, k).wait_send()
 
         def grid_step(n, carry):
             away = lax.div(n + 1, 2)
@@ -308,6 +317,10 @@
             @pl.when(n == 2)
             def _():
                 z_step(0, False)
+
+            @pl.when(n == 6)
+            def _():
+                z_step(3, True)
 
             return carry
 
@@ -361,20 +374,19 @@
         z_step(2, False)
         st3[z] = gather(st2, j, st2_s, st2_r, c_peer, chan_size)
         share(st3, z, st3_s, st3_r, z_peer, nz)
-        z_step(3, True)
         for r in range(1, NX):
             remote(
                 final.at[pl.ds(0, TP), :], mine.at[r], mine_s.at[r], mine_r.at[r], x_peer(r)
             ).wait_recv()
         for copy in sends:
             copy.wait_send()
-        z_sent(False)
-
-        for way in range(2):
+        z_sent((0, 1, 3))
+
+        for slot in range(3):
             for source in range(NX):
                 remote(
-                    zsend.at[way, 0, 0], edge.at[way, source], z_s.at[way, 0, 0],
-                    edge_r.at[way, source], beside(way, x_peer(0)),
+                    zsend.at[0, 0, 0], edge.at[slot, source], z_s.at[0, 0, 0],
+                    edge_r.at[slot, source], beside(0, x_peer(0), 1),
                 ).wait_recv()
         for r in range(NX):
             source = lax.rem(x + r, NX)
@@ -382,11 +394,12 @@
                 value = mine[r].astype(f32)
             else:
                 value = part[pl.ds(pl.multiple_of(chunk_row(0) + x * TP, TP), TP), :]
-            value = value + edge[0, source].astype(f32) + edge[1, source].astype(f32)
+            for slot in range(3):
+                value = value + edge[slot, source].astype(f32)
             column = pl.multiple_of(source * quarter, quarter)
             sky[:, pl.ds(column, quarter)] = value.astype(bf16)
         stacked[...] = gather(st3, z, st3_s, st3_r, z_peer, nz) / ngal
-        z_sent(True)
+        z_sent((2,))
 
     dma = pltpu.SemaphoreType.DMA
     scratch = [
@@ -404,8 +417,8 @@
         pltpu.VMEM((ngal, npix), bf16),
         pltpu.VMEM((shifts, npix), bf16),
         pltpu.VMEM((2, NX, far, TP, quarter), bf16),
-        pltpu.VMEM((2, NX, far - 1, TP, quarter), bf16),
-        pltpu.VMEM((2, NX, TP, quarter), bf16),
+        pltpu.VMEM((2, NX, 2, TP, quarter), bf16),
+        pltpu.VMEM((3, NX, TP, quarter), bf16),
         pltpu.VMEM((zpix, quarter), bf16),
         pltpu.VMEM((NX, TP, quarter), bf16),
         pltpu.VMEM((NX, 1, 2 * SW), f32),
@@ -415,7 +428,7 @@
     ]
     for shape in ((NX,), (3, NX), (chan_size,), (chan_size,), (NX,)):
         scratch += [dma(shape), dma(shape)]
-    scratch += [dma((2, NX, far)), dma((2, NX, far - 1)), dma((2, NX))]
+    scratch += [dma((2, NX, far)), dma((2, NX, 2)), dma((3, NX))]
     for shape in ((NX,), (NX,), (chan_size,), (nz,)):
         scratch += [dma(shape), dma(shape)]
     return kernel, scratch

time: 44.6 us -> 44.8 us (level)
  no operation moved by 1% of the time
where the time goes in v9:
time: 44.8 us; the launch traced here: 44.7 us
  Pallas kernels  42.2 us (94%)
  local copies, waits for them, and re-layouts  1.86 us (4%)
  between operations  0.69 us (2%)
    pallas_call x1, Pallas kernels, per_device(): pl.pallas_call(kernel, out_shape=(jax.ShapeDtypeStruct((TP, width), bf16)...  42.2 us
    unnamed x14, local copies, waits for them, and re-layouts  1.86 us

profile of v9, /device:TPU:1, one launch (start us, length us, event | category | flops | bytes accessed | tf_op | source)
XLA Modules:
  0.0 44.7 jit_solution(2684680903709838388)
XLA Ops:
  0.6 0.0 copy-start.3
  0.6 0.0 copy-start.5
  0.7 0.0 copy-start
  0.7 0.0 copy-start.1
  0.7 0.0 copy-start.2
  0.7 0.0 copy-start.4
  0.7 0.6 %copy-done.3 = s32[256]{0:T(256)S(1)} copy-done((s32[256]{0:T(256)S(1)}, s32[256]{0:T(256)}, u32[]{:S(2)}) %copy-start.3) | copy-done | bytes 1048
  1.3 0.0 copy-done.5
  1.3 0.0 copy-done
  1.4 0.0 copy-done.1
  1.4 0.0 copy-done.2
  1.4 0.0 copy-done.4
  1.4 42.2 %shard_map.95 = (bf16[64,1024]{1,0:T(8,128)(2,1)S(1)}, f32[1,128]{1,0:T(1,128)S(1)}) custom-call(bf16[512,1024]{1,0:T(8,128)(2,1)} %spec.1, f32[16,8192]{1,0:T(8,128)} %constant.2.clone.basis_in, f32[1,1024]{1,0:T(1,128)S(1)} %bitcast.7, s32[1,32]{1,0:T(1,128)S(1)} %bitcast.11, s32[1,512]{1,0:T(1,128)S(1)} %bitcast.8, bf16[1,16]{1,0:T(2,128)(2,1)S(1)} %bitcast.12, ...), custom_call_target="tpu_custom_call" | custom-call | tf_op jit(solution)/shard_map/pallas_call | solution.py:447
  43.5 0.7 %copy.12 = bf16[64,1024]{1,0:T(8,128)(2,1)} copy(bf16[64,1024]{1,0:T(8,128)(2,1)S(1)} %get-tuple-element.8) | data formatting | bytes 262144
  44.2 0.5 %copy.13 = f32[128]{0:T(128)} copy(f32[128]{0:T(128)S(1)} %bitcast.13) | data formatting | bytes 1024
Async XLA Ops:
  0.6 0.7 %copy-start.3 = (s32[256]{0:T(256)S(1)}, s32[256]{0:T(256)}, u32[]{:S(2)}) copy-start(s32[256]{0:T(256)} %param.14) | copy-start | bytes 3076
  0.6 0.7 %copy-start.5 = (bf16[16]{0:T(256)(128)(2,1)S(1)}, bf16[16]{0:T(256)(128)(2,1)}, u32[]{:S(2)}) copy-start(bf16[16]{0:T(256)(128)(2,1)} %param.12) | copy-start | bytes 100
  0.7 0.7 %copy-start = (f32[1024]{0:T(1024)S(1)}, f32[1024]{0:T(1024)}, u32[]{:S(2)}) copy-start(f32[1024]{0:T(1024)} %param.9) | copy-start | bytes 12292
  0.7 0.7 %copy-start.1 = (s32[512]{0:T(512)S(1)}, s32[512]{0:T(512)}, u32[]{:S(2)}) copy-start(s32[512]{0:T(512)} %param.11) | copy-start | bytes 6148
  0.7 0.7 %copy-start.2 = (s32[256]{0:T(256)S(1)}, s32[256]{0:T(256)}, u32[]{:S(2)}) copy-start(s32[256]{0:T(256)} %param.13) | copy-start | bytes 3076
  0.7 0.7 %copy-start.4 = (s32[32,1]{0,1:T(1,128)S(1)}, s32[32,1]{0,1:T(1,128)}, u32[]{:S(2)}) copy-start(s32[32,1]{0,1:T(1,128)} %param.10) | copy-start | bytes 388

commit v10 on v8

--- a/solution.py
+++ b/solution.py
@@ -50,7 +50,7 @@
     def kernel(
         spec, basis_in, weight, routes, offsets, taps, gal_pix, gal_chan,
         sky, stacked,
-        own, basis, pix, raw, gram, proj, coef, band, ripple, clean, part, pixel_hot, counts,
+        own, basis, pix, raw, gram, proj, coef, band, ripple, clean, part, rounded, pixel_hot, shift_hot,
         zsend, zrecv, edge, final, mine, st1, st2, st3,
         load_sem, pix_s, pix_r, raw_s, raw_r, gram_s, gram_r, proj_s, proj_r, coef_s, coef_r,
         z_s, z_r, edge_r, mine_s, mine_r, st1_s, st1_r, st2_s, st2_r, st3_s, st3_r,
@@ -181,16 +181,12 @@
         build_band(0)
 
         begin = gal_chan[...] - SW - (j * width + here)
-        shift_hot = (iota((shifts, ngal), 0) == quarter - 1 - begin).astype(f32).astype(bf16)
+        shift_hot[...] = (iota((shifts, ngal), 0) == quarter - 1 - begin).astype(f32).astype(bf16)
         gal_column = jnp.broadcast_to(gal_pix[...].astype(f32), (128, ngal)).T.astype(jnp.int32)
         for i in range(npix // 128):
             pixel_hot[:, 128 * i:128 * (i + 1)] = jnp.where(
                 gal_column - 128 * i == iota((ngal, 128), 1), 1.0, 0.0
             ).astype(bf16)
-        counts[...] = jnp.dot(
-            shift_hot, pixel_hot[...], preferred_element_type=f32
-        ).astype(bf16)
-
         for r in range(1, NX):
             remote(pix.at[0], pix.at[r], pix_s.at[r], pix_r.at[r], x_peer(r)).wait_recv()
             build_band(r)
@@ -297,9 +293,11 @@
         def grid_step(n, carry):
             away = lax.div(n + 1, 2)
             row = chunk_row(far + away - 2 * lax.rem(n, 2) * away)
-            part[pl.ds(row, zpix), :] = jnp.dot(
+            chunk = jnp.dot(
                 band[pl.ds(row, zpix), :], clean[...], preferred_element_type=f32
             )
+            part[pl.ds(row, zpix), :] = chunk
+            rounded[pl.ds(row, zpix), :] = chunk.astype(bf16)
 
             @pl.when(n == 0)
             def _():
@@ -328,9 +326,12 @@
 
         lax.fori_loop(0, nz, grid_step, 0)
 
+        picked = jnp.dot(
+            pixel_hot[...], rounded[...], preferred_element_type=f32
+        ).astype(bf16)
         wide = jnp.concatenate(
             [
-                jnp.dot(counts[...], part[...].astype(bf16), preferred_element_type=f32),
+                jnp.dot(shift_hot[...], picked, preferred_element_type=f32),
                 jnp.zeros((shifts, 512 - quarter), f32),
             ],
             axis=1,
@@ -348,7 +349,7 @@
 
         z_step(1, True)
         z_step(1, False)
-        final[...] = part[pl.ds(chunk_row(0), zpix), :].astype(bf16)
+        final[...] = rounded[pl.ds(chunk_row(0), zpix), :]
         for r in range(1, NX):
             row = pl.multiple_of(lax.rem(x + r, NX) * TP, TP)
             start(remote(
@@ -401,8 +402,9 @@
         pltpu.VMEM((NX * rows, quarter), f32),
         pltpu.VMEM((NX * rows, quarter), bf16),
         pltpu.VMEM((npix, quarter), f32),
+        pltpu.VMEM((npix, quarter), bf16),
         pltpu.VMEM((ngal, npix), bf16),
-        pltpu.VMEM((shifts, npix), bf16),
+        pltpu.VMEM((shifts, ngal), bf16),
         pltpu.VMEM((2, NX, far, TP, quarter), bf16),
         pltpu.VMEM((2, NX, far - 1, TP, quarter), bf16),
         pltpu.VMEM((2, NX, TP, quarter), bf16),

time: 44.6 us -> 44.8 us (level)
  no operation moved by 1% of the time
where the time goes in v10:
time: 44.8 us; the launch traced here: 44.6 us
  Pallas kernels  42.1 us (94%)
  local copies, waits for them, and re-layouts  1.86 us (4%)
  between operations  0.69 us (2%)
    pallas_call x1, Pallas kernels, per_device(): pl.pallas_call(kernel, out_shape=(jax.ShapeDtypeStruct((TP, width), bf16)...  42.1 us
    unnamed x14, local copies, waits for them, and re-layouts  1.86 us

profile of v10, /device:TPU:1, one launch (start us, length us, event | category | flops | bytes accessed | tf_op | source)
XLA Modules:
  0.0 44.6 jit_solution(16998560160083732458)
XLA Ops:
  0.6 0.0 copy-start.3
  0.6 0.0 copy-start.5
  0.7 0.0 copy-start
  0.7 0.0 copy-start.1
  0.7 0.0 copy-start.2
  0.7 0.0 copy-start.4
  0.7 0.6 %copy-done.3 = s32[256]{0:T(256)S(1)} copy-done((s32[256]{0:T(256)S(1)}, s32[256]{0:T(256)}, u32[]{:S(2)}) %copy-start.3) | copy-done | bytes 1048
  1.3 0.0 copy-done.5
  1.3 0.0 copy-done
  1.4 0.0 copy-done.1
  1.4 0.0 copy-done.2
  1.4 0.0 copy-done.4
  1.4 42.1 %shard_map.95 = (bf16[64,1024]{1,0:T(8,128)(2,1)S(1)}, f32[1,128]{1,0:T(1,128)S(1)}) custom-call(bf16[512,1024]{1,0:T(8,128)(2,1)} %spec.1, f32[16,8192]{1,0:T(8,128)} %constant.2.clone.basis_in, f32[1,1024]{1,0:T(1,128)S(1)} %bitcast.7, s32[1,32]{1,0:T(1,128)S(1)} %bitcast.11, s32[1,512]{1,0:T(1,128)S(1)} %bitcast.8, bf16[1,16]{1,0:T(2,128)(2,1)S(1)} %bitcast.12, ...), custom_call_target="tpu_custom_call" | custom-call | tf_op jit(solution)/shard_map/pallas_call | solution.py:436
  43.5 0.7 %copy.12 = bf16[64,1024]{1,0:T(8,128)(2,1)} copy(bf16[64,1024]{1,0:T(8,128)(2,1)S(1)} %get-tuple-element.8) | data formatting | bytes 262144
  44.1 0.5 %copy.13 = f32[128]{0:T(128)} copy(f32[128]{0:T(128)S(1)} %bitcast.13) | data formatting | bytes 1024
Async XLA Ops:
  0.6 0.7 %copy-start.3 = (s32[256]{0:T(256)S(1)}, s32[256]{0:T(256)}, u32[]{:S(2)}) copy-start(s32[256]{0:T(256)} %param.14) | copy-start | bytes 3076
  0.6 0.7 %copy-start.5 = (bf16[16]{0:T(256)(128)(2,1)S(1)}, bf16[16]{0:T(256)(128)(2,1)}, u32[]{:S(2)}) copy-start(bf16[16]{0:T(256)(128)(2,1)} %param.12) | copy-start | bytes 100
  0.7 0.7 %copy-start = (f32[1024]{0:T(1024)S(1)}, f32[1024]{0:T(1024)}, u32[]{:S(2)}) copy-start(f32[1024]{0:T(1024)} %param.9) | copy-start | bytes 12292
  0.7 0.7 %copy-start.1 = (s32[512]{0:T(512)S(1)}, s32[512]{0:T(512)}, u32[]{:S(2)}) copy-start(s32[512]{0:T(512)} %param.11) | copy-start | bytes 6148
  0.7 0.7 %copy-start.2 = (s32[256]{0:T(256)S(1)}, s32[256]{0:T(256)}, u32[]{:S(2)}) copy-start(s32[256]{0:T(256)} %param.13) | copy-start | bytes 3076
  0.7 0.7 %copy-start.4 = (s32[32,1]{0,1:T(1,128)S(1)}, s32[32,1]{0,1:T(1,128)}, u32[]{:S(2)}) copy-start(s32[32,1]{0,1:T(1,128)} %param.10) | copy-start | bytes 388

commit v11 on v10

--- a/solution.py
+++ b/solution.py
@@ -50,9 +50,9 @@
     def kernel(
         spec, basis_in, weight, routes, offsets, taps, gal_pix, gal_chan,
         sky, stacked,
-        own, basis, pix, raw, gram, proj, coef, band, ripple, clean, part, rounded, pixel_hot, shift_hot,
+        own, basis, pix, raw, relay, gram, proj, coef, band, ripple, clean, part, rounded, pixel_hot, shift_hot,
         zsend, zrecv, edge, final, mine, st1, st2, st3,
-        load_sem, pix_s, pix_r, raw_s, raw_r, gram_s, gram_r, proj_s, proj_r, coef_s, coef_r,
+        load_sem, pix_s, pix_r, raw_s, raw_r, relay_s, relay_r, next_s, next_r, gram_s, gram_r, proj_s, proj_r, coef_s, coef_r,
         z_s, z_r, edge_r, mine_s, mine_r, st1_s, st1_r, st2_s, st2_r, st3_s, st3_r,
     ):
         tm = lax.axis_index("tm")
@@ -119,14 +119,31 @@
 
         def raw_copy(r, piece):
             column = pl.multiple_of(lax.rem(x + r, NX) * quarter, quarter)
-            low, high = ((0, late), (late, rows), (0, rows))[piece]
+            low, high = ((0, late), (late, rows))[piece]
             return remote(
                 spec.at[low:high, pl.ds(column, quarter)], raw.at[NX - r, low:high],
                 raw_s.at[piece, r], raw_r.at[piece, NX - r], x_peer(r),
             )
 
-        for r, piece in ((2, 2), (1, 0), (3, 0)):
-            start(raw_copy(r, piece))
+        mid = rows // 2
+        across = pl.multiple_of(lax.rem(x + 2, NX) * quarter, quarter)
+
+        def relay_copy(way):
+            return remote(
+                spec.at[way * mid:(way + 1) * mid, pl.ds(across, quarter)], relay.at[way],
+                relay_s.at[way], relay_r.at[way], x_peer((1, 3)[way]),
+            )
+
+        def next_copy(way):
+            return remote(
+                relay.at[way], raw.at[2, way * mid:(way + 1) * mid], next_s.at[way],
+                next_r.at[way], x_peer((1, 3)[way]),
+            )
+
+        for way in range(2):
+            start(relay_copy(way))
+        for r in (1, 3):
+            start(raw_copy(r, 0))
 
         loads[1].wait()
         weighted = basis[...] * weight[...]
@@ -190,6 +207,10 @@
         for r in range(1, NX):
             remote(pix.at[0], pix.at[r], pix_s.at[r], pix_r.at[r], x_peer(r)).wait_recv()
             build_band(r)
+            if r == 1:
+                for way in range(2):
+                    relay_copy(way).wait_recv()
+                    start(next_copy(way))
 
         for r in range(1, chan_size):
             remote(gram.at[0], gram.at[r], gram_s.at[r], gram_r.at[r], c_peer(r)).wait_recv()
@@ -244,8 +265,11 @@
         for r in (1, 3, 2):
             remote(coef.at[0], coef.at[r], coef_s.at[r], coef_r.at[r], x_peer(r)).wait_recv()
             fit_slot(r)
-        for r, pieces in ((2, (2,)), (1, (0, 1)), (3, (0, 1))):
-            for piece in pieces:
+        for way in range(2):
+            next_copy(way).wait_recv()
+        clean_slot(2, raw[2])
+        for r in (1, 3):
+            for piece in range(2):
                 raw_copy(NX - r, piece).wait_recv()
             clean_slot(r, raw[r])
 
@@ -395,6 +419,7 @@
         pltpu.VMEM((MODES, width), f32),
         pltpu.VMEM((NX, 1, rows), jnp.int32),
         pltpu.VMEM((NX, rows, quarter), bf16),
+        pltpu.VMEM((2, rows // 2, quarter), bf16),
         pltpu.VMEM((chan_size, MODES, 128), f32),
         pltpu.VMEM((chan_size, MODES, rows), f32),
         pltpu.VMEM((NX, MODES, rows), f32),
@@ -415,7 +440,7 @@
         pltpu.VMEM((nz, 1, 2 * SW), f32),
         dma((2,)),
     ]
-    for shape in ((NX,), (3, NX), (chan_size,), (chan_size,), (NX,)):
+    for shape in ((NX,), (2, NX), (2,), (2,), (chan_size,), (chan_size,), (NX,)):
         scratch += [dma(shape), dma(shape)]
     scratch += [dma((2, NX, far)), dma((2, NX, far - 1)), dma((2, NX))]
     for shape in ((NX,), (NX,), (chan_size,), (nz,)):

time: 44.8 us -> 44.8 us (level)
  no operation moved by 1% of the time
where the time goes in v11:
time: 44.8 us; the launch traced here: 44.7 us
  Pallas kernels  42.1 us (94%)
  local copies, waits for them, and re-layouts  1.86 us (4%)
  between operations  0.69 us (2%)
    pallas_call x1, Pallas kernels, per_device(): pl.pallas_call(kernel, out_shape=(jax.ShapeDtypeStruct((TP, width), bf16)...  42.1 us
    unnamed x14, local copies, waits for them, and re-layouts  1.86 us

profile of v11, /device:TPU:1, one launch (start us, length us, event | category | flops | bytes accessed | tf_op | source)
XLA Modules:
  0.0 44.7 jit_solution(6912987168600284478)
XLA Ops:
  0.6 0.0 copy-start.3
  0.6 0.0 copy-start.5
  0.7 0.0 copy-start
  0.7 0.0 copy-start.1
  0.7 0.0 copy-start.2
  0.7 0.0 copy-start.4
  0.7 0.6 %copy-done.3 = s32[256]{0:T(256)S(1)} copy-done((s32[256]{0:T(256)S(1)}, s32[256]{0:T(256)}, u32[]{:S(2)}) %copy-start.3) | copy-done | bytes 1048
  1.3 0.0 copy-done.5
  1.3 0.0 copy-done
  1.4 0.0 copy-done.1
  1.4 0.0 copy-done.2
  1.4 0.0 copy-done.4
  1.4 42.1 %shard_map.95 = (bf16[64,1024]{1,0:T(8,128)(2,1)S(1)}, f32[1,128]{1,0:T(1,128)S(1)}) custom-call(bf16[512,1024]{1,0:T(8,128)(2,1)} %spec.1, f32[16,8192]{1,0:T(8,128)} %constant.2.clone.basis_in, f32[1,1024]{1,0:T(1,128)S(1)} %bitcast.7, s32[1,32]{1,0:T(1,128)S(1)} %bitcast.11, s32[1,512]{1,0:T(1,128)S(1)} %bitcast.8, bf16[1,16]{1,0:T(2,128)(2,1)S(1)} %bitcast.12, ...), custom_call_target="tpu_custom_call" | custom-call | tf_op jit(solution)/shard_map/pallas_call | solution.py:461
  43.5 0.7 %copy.12 = bf16[64,1024]{1,0:T(8,128)(2,1)} copy(bf16[64,1024]{1,0:T(8,128)(2,1)S(1)} %get-tuple-element.8) | data formatting | bytes 262144
  44.2 0.5 %copy.13 = f32[128]{0:T(128)} copy(f32[128]{0:T(128)S(1)} %bitcast.13) | data formatting | bytes 1024
Async XLA Ops:
  0.6 0.7 %copy-start.3 = (s32[256]{0:T(256)S(1)}, s32[256]{0:T(256)}, u32[]{:S(2)}) copy-start(s32[256]{0:T(256)} %param.14) | copy-start | bytes 3076
  0.6 0.7 %copy-start.5 = (bf16[16]{0:T(256)(128)(2,1)S(1)}, bf16[16]{0:T(256)(128)(2,1)}, u32[]{:S(2)}) copy-start(bf16[16]{0:T(256)(128)(2,1)} %param.12) | copy-start | bytes 100
  0.7 0.7 %copy-start = (f32[1024]{0:T(1024)S(1)}, f32[1024]{0:T(1024)}, u32[]{:S(2)}) copy-start(f32[1024]{0:T(1024)} %param.9) | copy-start | bytes 12292
  0.7 0.7 %copy-start.1 = (s32[512]{0:T(512)S(1)}, s32[512]{0:T(512)}, u32[]{:S(2)}) copy-start(s32[512]{0:T(512)} %param.11) | copy-start | bytes 6148
  0.7 0.7 %copy-start.2 = (s32[256]{0:T(256)S(1)}, s32[256]{0:T(256)}, u32[]{:S(2)}) copy-start(s32[256]{0:T(256)} %param.13) | copy-start | bytes 3076
  0.7 0.7 %copy-start.4 = (s32[32,1]{0,1:T(1,128)S(1)}, s32[32,1]{0,1:T(1,128)}, u32[]{:S(2)}) copy-start(s32[32,1]{0,1:T(1,128)} %param.10) | copy-start | bytes 388

commit v12 on v9

--- a/solution.py
+++ b/solution.py
@@ -50,7 +50,7 @@
     def kernel(
         spec, basis_in, weight, routes, offsets, taps, gal_pix, gal_chan,
         sky, stacked,
-        own, basis, pix, raw, gram, proj, coef, band, ripple, clean, part, pixel_hot, counts,
+        own, basis, pix, raw, gram, proj, coef, band, ripple, clean, part, rounded, pixel_hot, shift_hot,
         zsend, zrecv, edge, final, mine, st1, st2, st3,
         load_sem, pix_s, pix_r, raw_s, raw_r, gram_s, gram_r, proj_s, proj_r, coef_s, coef_r,
         z_s, z_r, edge_r, mine_s, mine_r, st1_s, st1_r, st2_s, st2_r, st3_s, st3_r,
@@ -185,16 +185,12 @@
         build_band(0)
 
         begin = gal_chan[...] - SW - (j * width + here)
-        shift_hot = (iota((shifts, ngal), 0) == quarter - 1 - begin).astype(f32).astype(bf16)
+        shift_hot[...] = (iota((shifts, ngal), 0) == quarter - 1 - begin).astype(f32).astype(bf16)
         gal_column = jnp.broadcast_to(gal_pix[...].astype(f32), (128, ngal)).T.astype(jnp.int32)
         for i in range(npix // 128):
             pixel_hot[:, 128 * i:128 * (i + 1)] = jnp.where(
                 gal_column - 128 * i == iota((ngal, 128), 1), 1.0, 0.0
             ).astype(bf16)
-        counts[...] = jnp.dot(
-            shift_hot, pixel_hot[...], preferred_element_type=f32
-        ).astype(bf16)
-
         for r in range(1, NX):
             remote(pix.at[0], pix.at[r], pix_s.at[r], pix_r.at[r], x_peer(r)).wait_recv()
             build_band(r)
@@ -306,9 +302,11 @@
         def grid_step(n, carry):
             away = lax.div(n + 1, 2)
             row = chunk_row(far + away - 2 * lax.rem(n, 2) * away)
-            part[pl.ds(row, zpix), :] = jnp.dot(
+            chunk = jnp.dot(
                 band[pl.ds(row, zpix), :], clean[...], preferred_element_type=f32
             )
+            part[pl.ds(row, zpix), :] = chunk
+            rounded[pl.ds(row, zpix), :] = chunk.astype(bf16)
 
             @pl.when(n == 0)
             def _():
@@ -341,9 +339,12 @@
 
         lax.fori_loop(0, nz, grid_step, 0)
 
+        picked = jnp.dot(
+            pixel_hot[...], rounded[...], preferred_element_type=f32
+        ).astype(bf16)
         wide = jnp.concatenate(
             [
-                jnp.dot(counts[...], part[...].astype(bf16), preferred_element_type=f32),
+                jnp.dot(shift_hot[...], picked, preferred_element_type=f32),
                 jnp.zeros((shifts, 512 - quarter), f32),
             ],
             axis=1,
@@ -361,7 +362,7 @@
 
         z_step(1, True)
         z_step(1, False)
-        final[...] = part[pl.ds(chunk_row(0), zpix), :].astype(bf16)
+        final[...] = rounded[pl.ds(chunk_row(0), zpix), :]
         for r in range(1, NX):
             row = pl.multiple_of(lax.rem(x + r, NX) * TP, TP)
             start(remote(
@@ -414,8 +415,9 @@
         pltpu.VMEM((NX * rows, quarter), f32),
         pltpu.VMEM((NX * rows, quarter), bf16),
         pltpu.VMEM((npix, quarter), f32),
+        pltpu.VMEM((npix, quarter), bf16),
         pltpu.VMEM((ngal, npix), bf16),
-        pltpu.VMEM((shifts, npix), bf16),
+        pltpu.VMEM((shifts, ngal), bf16),
         pltpu.VMEM((2, NX, far, TP, quarter), bf16),
         pltpu.VMEM((2, NX, 2, TP, quarter), bf16),
         pltpu.VMEM((3, NX, TP, quarter), bf16),

time: 44.8 us -> 45 us (level)
  no operation moved by 1% of the time
where the time goes in v12:
time: 45 us; the launch traced here: 44.9 us
  Pallas kernels  42.3 us (94%)
  local copies, waits for them, and re-layouts  1.86 us (4%)
  between operations  0.69 us (2%)
    pallas_call x1, Pallas kernels, per_device(): pl.pallas_call(kernel, out_shape=(jax.ShapeDtypeStruct((TP, width), bf16)...  42.3 us
    unnamed x14, local copies, waits for them, and re-layouts  1.86 us

profile of v12, /device:TPU:1, one launch (start us, length us, event | category | flops | bytes accessed | tf_op | source)
XLA Modules:
  0.0 44.9 jit_solution(18028732338749447988)
XLA Ops:
  0.6 0.0 copy-start.3
  0.6 0.0 copy-start.5
  0.7 0.0 copy-start
  0.7 0.0 copy-start.1
  0.7 0.0 copy-start.2
  0.7 0.0 copy-start.4
  0.7 0.6 %copy-done.3 = s32[256]{0:T(256)S(1)} copy-done((s32[256]{0:T(256)S(1)}, s32[256]{0:T(256)}, u32[]{:S(2)}) %copy-start.3) | copy-done | bytes 1048
  1.3 0.0 copy-done.5
  1.3 0.0 copy-done
  1.4 0.0 copy-done.1
  1.4 0.0 copy-done.2
  1.4 0.0 copy-done.4
  1.4 42.3 %shard_map.95 = (bf16[64,1024]{1,0:T(8,128)(2,1)S(1)}, f32[1,128]{1,0:T(1,128)S(1)}) custom-call(bf16[512,1024]{1,0:T(8,128)(2,1)} %spec.1, f32[16,8192]{1,0:T(8,128)} %constant.2.clone.basis_in, f32[1,1024]{1,0:T(1,128)S(1)} %bitcast.7, s32[1,32]{1,0:T(1,128)S(1)} %bitcast.11, s32[1,512]{1,0:T(1,128)S(1)} %bitcast.8, bf16[1,16]{1,0:T(2,128)(2,1)S(1)} %bitcast.12, ...), custom_call_target="tpu_custom_call" | custom-call | tf_op jit(solution)/shard_map/pallas_call | solution.py:449
  43.7 0.7 %copy.12 = bf16[64,1024]{1,0:T(8,128)(2,1)} copy(bf16[64,1024]{1,0:T(8,128)(2,1)S(1)} %get-tuple-element.8) | data formatting | bytes 262144
  44.4 0.5 %copy.13 = f32[128]{0:T(128)} copy(f32[128]{0:T(128)S(1)} %bitcast.13) | data formatting | bytes 1024
Async XLA Ops:
  0.6 0.7 %copy-start.3 = (s32[256]{0:T(256)S(1)}, s32[256]{0:T(256)}, u32[]{:S(2)}) copy-start(s32[256]{0:T(256)} %param.14) | copy-start | bytes 3076
  0.6 0.7 %copy-start.5 = (bf16[16]{0:T(256)(128)(2,1)S(1)}, bf16[16]{0:T(256)(128)(2,1)}, u32[]{:S(2)}) copy-start(bf16[16]{0:T(256)(128)(2,1)} %param.12) | copy-start | bytes 100
  0.7 0.7 %copy-start = (f32[1024]{0:T(1024)S(1)}, f32[1024]{0:T(1024)}, u32[]{:S(2)}) copy-start(f32[1024]{0:T(1024)} %param.9) | copy-start | bytes 12292
  0.7 0.7 %copy-start.1 = (s32[512]{0:T(512)S(1)}, s32[512]{0:T(512)}, u32[]{:S(2)}) copy-start(s32[512]{0:T(512)} %param.11) | copy-start | bytes 6148
  0.7 0.7 %copy-start.2 = (s32[256]{0:T(256)S(1)}, s32[256]{0:T(256)}, u32[]{:S(2)}) copy-start(s32[256]{0:T(256)} %param.13) | copy-start | bytes 3076
  0.7 0.7 %copy-start.4 = (s32[32,1]{0,1:T(1,128)S(1)}, s32[32,1]{0,1:T(1,128)}, u32[]{:S(2)}) copy-start(s32[32,1]{0,1:T(1,128)} %param.10) | copy-start | bytes 388

commit v13 on v10

--- a/solution.py
+++ b/solution.py
@@ -53,7 +53,7 @@
         own, basis, pix, raw, gram, proj, coef, band, ripple, clean, part, rounded, pixel_hot, shift_hot,
         zsend, zrecv, edge, final, mine, st1, st2, st3,
         load_sem, pix_s, pix_r, raw_s, raw_r, gram_s, gram_r, proj_s, proj_r, coef_s, coef_r,
-        z_s, z_r, edge_r, mine_s, mine_r, st1_s, st1_r, st2_s, st2_r, st3_s, st3_r,
+        z_s, z_r, edge_s, edge_r, mine_s, mine_r, st1_s, st1_r, st2_s, st2_r, st3_s, st3_r,
     ):
         tm = lax.axis_index("tm")
         j = lax.axis_index("chan")
@@ -252,43 +252,49 @@
         def chunk_row(step):
             return pl.multiple_of(lax.rem(z + step + 2 * nz, nz) * zpix, zpix)
 
-        def part_tile(step, tile):
-            row = pl.multiple_of(chunk_row(step) + tile * TP, TP)
-            return part[pl.ds(row, TP), :]
+        def part_half(step, which):
+            row = pl.multiple_of(chunk_row(step) + which * 2 * TP, 2 * TP)
+            return part[pl.ds(row, 2 * TP), :]
 
         sign = (1, -1)
 
-        def hops(way, tile):
-            return far if tile // 2 == way else far - 1
-
-        def z_copy(way, tile, k):
-            if k < hops(way, tile) - 1:
-                target, recv_sem = zrecv.at[way, tile, k], z_r.at[way, tile, k]
-                peer = z_peer((1, nz - 1)[way])
-            else:
-                target, recv_sem = edge.at[way, x], edge_r.at[way, x]
-                peer = beside(way, (z * NX + tile, j))
-            return remote(
-                zsend.at[way, tile, k], target, z_s.at[way, tile, k], recv_sem, peer
-            )
+        def z_copies(way, long, k):
+            hops = far if long else far - 1
+            kind = 0 if long else 1
+            source = zsend.at[way, kind, k]
+            if k < hops - 1:
+                return [remote(
+                    source, zrecv.at[way, kind, k], z_s.at[way, kind, k], z_r.at[way, kind, k],
+                    z_peer((1, nz - 1)[way]),
+                )]
+            first = 2 * (way if long else 1 - way)
+            return [
+                remote(
+                    source.at[i * TP:(i + 1) * TP], edge.at[way, x], edge_s.at[way, first + i],
+                    edge_r.at[way, x], beside(way, (z * NX + first + i, j)),
+                )
+                for i in range(2)
+            ]
 
         def z_step(k, long):
-            for lane in range(2):
-                for way in range(2):
-                    tile = 2 * (way if long else 1 - way) + lane
-                    value = part_tile(sign[way] * (hops(way, tile) - k), tile)
-                    if k:
-                        z_copy(way, tile, k - 1).wait_recv()
-                        value = value + zrecv[way, tile, k - 1].astype(f32)
-                    zsend[way, tile, k] = value.astype(bf16)
-                    z_copy(way, tile, k).start()
+            hops = far if long else far - 1
+            kind = 0 if long else 1
+            for way in range(2):
+                value = part_half(sign[way] * (hops - k), way if long else 1 - way)
+                if k:
+                    z_copies(way, long, k - 1)[0].wait_recv()
+                    value = value + zrecv[way, kind, k - 1].astype(f32)
+                zsend[way, kind, k] = value.astype(bf16)
+                for copy in z_copies(way, long, k):
+                    copy.start()
 
         def z_sent(last):
             for way in range(2):
-                for tile in range(NX):
-                    count = hops(way, tile)
-                    for k in (count - 1,) if last else range(count - 1):
-                        z_copy(way, tile, k).wait_send()
+                for long in (True, False):
+                    hops = far if long else far - 1
+                    for k in (hops - 1,) if last else range(hops - 1):
+                        for copy in z_copies(way, long, k):
+                            copy.wait_send()
 
         def grid_step(n, carry):
             away = lax.div(n + 1, 2)
@@ -374,7 +380,7 @@
         for way in range(2):
             for source in range(NX):
                 remote(
-                    zsend.at[way, 0, 0], edge.at[way, source], z_s.at[way, 0, 0],
+                    zsend.at[way, 0, 0, 0:TP], edge.at[way, source], edge_s.at[way, source],
                     edge_r.at[way, source], beside(way, x_peer(0)),
                 ).wait_recv()
         for r in range(NX):
@@ -405,8 +411,8 @@
         pltpu.VMEM((npix, quarter), bf16),
         pltpu.VMEM((ngal, npix), bf16),
         pltpu.VMEM((shifts, ngal), bf16),
-        pltpu.VMEM((2, NX, far, TP, quarter), bf16),
-        pltpu.VMEM((2, NX, far - 1, TP, quarter), bf16),
+        pltpu.VMEM((2, 2, far, 2 * TP, quarter), bf16),
+        pltpu.VMEM((2, 2, far - 1, 2 * TP, quarter), bf16),
         pltpu.VMEM((2, NX, TP, quarter), bf16),
         pltpu.VMEM((zpix, quarter), bf16),
         pltpu.VMEM((NX, TP, quarter), bf16),
@@ -417,7 +423,7 @@
     ]
     for shape in ((NX,), (3, NX), (chan_size,), (chan_size,), (NX,)):
         scratch += [dma(shape), dma(shape)]
-    scratch += [dma((2, NX, far)), dma((2, NX, far - 1)), dma((2, NX))]
+    scratch += [dma((2, 2, far)), dma((2, 2, far - 1)), dma((2, NX)), dma((2, NX))]
     for shape in ((NX,), (NX,), (chan_size,), (nz,)):
         scratch += [dma(shape), dma(shape)]
     return kernel, scratch

time: 44.8 us -> 44.6 us (level)
  no operation moved by 1% of the time
where the time goes in v13:
time: 44.6 us; the launch traced here: 44.4 us
  Pallas kernels  41.9 us (94%)
  local copies, waits for them, and re-layouts  1.86 us (4%)
  between operations  0.69 us (2%)
    pallas_call x1, Pallas kernels, per_device(): pl.pallas_call(kernel, out_shape=(jax.ShapeDtypeStruct((TP, width), bf16)...  41.9 us
    unnamed x14, local copies, waits for them, and re-layouts  1.86 us

profile of v13, /device:TPU:1, one launch (start us, length us, event | category | flops | bytes accessed | tf_op | source)
XLA Modules:
  0.0 44.4 jit_solution(8948090340327525252)
XLA Ops:
  0.6 0.0 copy-start.3
  0.6 0.0 copy-start.5
  0.7 0.0 copy-start
  0.7 0.0 copy-start.1
  0.7 0.0 copy-start.2
  0.7 0.0 copy-start.4
  0.7 0.6 %copy-done.3 = s32[256]{0:T(256)S(1)} copy-done((s32[256]{0:T(256)S(1)}, s32[256]{0:T(256)}, u32[]{:S(2)}) %copy-start.3) | copy-done | bytes 1048
  1.3 0.0 copy-done.5
  1.3 0.0 copy-done
  1.4 0.0 copy-done.1
  1.4 0.0 copy-done.2
  1.4 0.0 copy-done.4
  1.4 41.9 %shard_map.95 = (bf16[64,1024]{1,0:T(8,128)(2,1)S(1)}, f32[1,128]{1,0:T(1,128)S(1)}) custom-call(bf16[512,1024]{1,0:T(8,128)(2,1)} %spec.1, f32[16,8192]{1,0:T(8,128)} %constant.2.clone.basis_in, f32[1,1024]{1,0:T(1,128)S(1)} %bitcast.7, s32[1,32]{1,0:T(1,128)S(1)} %bitcast.11, s32[1,512]{1,0:T(1,128)S(1)} %bitcast.8, bf16[1,16]{1,0:T(2,128)(2,1)S(1)} %bitcast.12, ...), custom_call_target="tpu_custom_call" | custom-call | tf_op jit(solution)/shard_map/pallas_call | solution.py:442
  43.3 0.7 %copy.12 = bf16[64,1024]{1,0:T(8,128)(2,1)} copy(bf16[64,1024]{1,0:T(8,128)(2,1)S(1)} %get-tuple-element.8) | data formatting | bytes 262144
  43.9 0.5 %copy.13 = f32[128]{0:T(128)} copy(f32[128]{0:T(128)S(1)} %bitcast.13) | data formatting | bytes 1024
Async XLA Ops:
  0.6 0.7 %copy-start.3 = (s32[256]{0:T(256)S(1)}, s32[256]{0:T(256)}, u32[]{:S(2)}) copy-start(s32[256]{0:T(256)} %param.14) | copy-start | bytes 3076
  0.6 0.7 %copy-start.5 = (bf16[16]{0:T(256)(128)(2,1)S(1)}, bf16[16]{0:T(256)(128)(2,1)}, u32[]{:S(2)}) copy-start(bf16[16]{0:T(256)(128)(2,1)} %param.12) | copy-start | bytes 100
  0.7 0.7 %copy-start = (f32[1024]{0:T(1024)S(1)}, f32[1024]{0:T(1024)}, u32[]{:S(2)}) copy-start(f32[1024]{0:T(1024)} %param.9) | copy-start | bytes 12292
  0.7 0.7 %copy-start.1 = (s32[512]{0:T(512)S(1)}, s32[512]{0:T(512)}, u32[]{:S(2)}) copy-start(s32[512]{0:T(512)} %param.11) | copy-start | bytes 6148
  0.7 0.7 %copy-start.2 = (s32[256]{0:T(256)S(1)}, s32[256]{0:T(256)}, u32[]{:S(2)}) copy-start(s32[256]{0:T(256)} %param.13) | copy-start | bytes 3076
  0.7 0.7 %copy-start.4 = (s32[32,1]{0,1:T(1,128)S(1)}, s32[32,1]{0,1:T(1,128)}, u32[]{:S(2)}) copy-start(s32[32,1]{0,1:T(1,128)} %param.10) | copy-start | bytes 388
